TPU v7x, 256 devices: a whole 4x4x8 slice. The times are simulated.
256 devices in a mesh: dp: 4 (over x_lo, core), ctx: 64 (over x_hi, z, y).
Axes of the slice: x: 4 (x_hi: 2, x_lo: 2; x = x_hi * 2 + x_lo), y: 4, z: 8, core: 2. Of those that a mesh axis runs over, the one named last changes fastest.
Arguments:
- query_gate: bfloat16 [8192, 4096], P('ctx', 'dp'), may hold values from -6 to 6
- key_gate: bfloat16 [8192, 4096], P('ctx', 'dp'), may hold values from -6 to 6
- value_gate: bfloat16 [8192, 4096], P('ctx', 'dp'), may hold values from -6 to 6
- out_grad: bfloat16 [8192, 4096], P('ctx', 'dp'), may hold values from -6 to 6
- filter_taps: float32 [8192, 4096], P('ctx', 'dp'), may hold values from -0.0625 to 0.0625
- skip: float32 [4096], P('dp'), may hold values from -6 to 6
Outputs:
- grad_query: bfloat16 [8192, 4096], P('ctx', 'dp')
- grad_key: bfloat16 [8192, 4096], P('ctx', 'dp')
- grad_value: bfloat16 [8192, 4096], P('ctx', 'dp')
- grad_filter: float32 [8192, 4096], P('ctx', 'dp')
- grad_skip: float32 [4096], P('dp')
All inputs are finite; a program needn't handle non-finite values.
Results may differ from a plain program's by a relative error of at most 0.001.
Values sent between devices are 32-bit elements; how exact they have to be, the bound alone decides.
A program may use at most 64 MiB of HBM per device.

v0:
```python
import math

import jax
import jax.numpy as jnp
from jax import lax
from jax.sharding import PartitionSpec as P

exact_mode = lax.Precision.HIGHEST


def angle_pair(first_ids, second_ids, period):
    product_ids = first_ids[:, None] * second_ids[None, :] % period
    angles = product_ids.astype(jnp.float32) * (2.0 * math.pi / period)
    return (jnp.cos(angles), jnp.sin(angles))


def block_section(block, position):
    shards = block.shape[0]
    stride = block.shape[1]
    channels = block.shape[2]
    period = 2 * shards * shards * stride
    cos_blocks, sin_blocks = angle_pair(jnp.arange(2 * shards), jnp.arange(shards), 2 * shards)
    local_pos = position * stride + jnp.arange(stride, dtype=jnp.int32)
    cos_twist, sin_twist = angle_pair(jnp.arange(2 * shards), local_pos, period)
    cos_twist = cos_twist[:, :, None]
    sin_twist = sin_twist[:, :, None]
    flattened = block.reshape(shards, stride * channels)
    real_part = jnp.dot(cos_blocks, flattened, precision=exact_mode).reshape(
        2 * shards, stride, channels
    )
    imag_part = -jnp.dot(sin_blocks, flattened, precision=exact_mode).reshape(
        2 * shards, stride, channels
    )
    return (
        real_part * cos_twist + imag_part * sin_twist,
        imag_part * cos_twist - real_part * sin_twist,
    )


def finish_section(real_in, imag_in):
    local_len = real_in.shape[1]
    cos_local, sin_local = angle_pair(jnp.arange(local_len), jnp.arange(local_len), local_len)
    real_out = jnp.einsum("kr,jrw->jkw", cos_local, real_in, precision=exact_mode) + jnp.einsum(
        "kr,jrw->jkw", sin_local, imag_in, precision=exact_mode
    )
    imag_out = jnp.einsum("kr,jrw->jkw", cos_local, imag_in, precision=exact_mode) - jnp.einsum(
        "kr,jrw->jkw", sin_local, real_in, precision=exact_mode
    )
    return (real_out, imag_out)


def as_blocks(signal, shards):
    return signal.reshape(shards, signal.shape[0] // shards, signal.shape[1])


def forward_three(first_sig, second_sig, third_sig):
    shards = lax.axis_size("ctx")
    position = lax.axis_index("ctx")
    blocks = (
        lax.all_to_all(
            as_blocks(first_sig, shards), "ctx", split_axis=0, concat_axis=0, tiled=True
        ),
        lax.all_to_all(
            as_blocks(second_sig, shards), "ctx", split_axis=0, concat_axis=0, tiled=True
        ),
        lax.all_to_all(
            as_blocks(third_sig, shards), "ctx", split_axis=0, concat_axis=0, tiled=True
        ),
    )
    first_tw = block_section(blocks[0], position)
    second_tw = block_section(blocks[1], position)
    third_tw = block_section(blocks[2], position)
    spread = (
        lax.all_to_all(first_tw[0], "ctx", split_axis=0, concat_axis=1, tiled=True),
        lax.all_to_all(first_tw[1], "ctx", split_axis=0, concat_axis=1, tiled=True),
        lax.all_to_all(second_tw[0], "ctx", split_axis=0, concat_axis=1, tiled=True),
        lax.all_to_all(second_tw[1], "ctx", split_axis=0, concat_axis=1, tiled=True),
        lax.all_to_all(third_tw[0], "ctx", split_axis=0, concat_axis=1, tiled=True),
        lax.all_to_all(third_tw[1], "ctx", split_axis=0, concat_axis=1, tiled=True),
    )
    return (
        finish_section(spread[0], spread[1]),
        finish_section(spread[2], spread[3]),
        finish_section(spread[4], spread[5]),
    )


def inverse_blocks(first_spec, second_spec, third_spec):
    shards = lax.axis_size("ctx")
    position = lax.axis_index("ctx")
    local_len = first_spec[0].shape[1]
    stride = local_len // shards
    period = 2 * shards * local_len
    cos_local, sin_local = angle_pair(jnp.arange(local_len), jnp.arange(local_len), local_len)
    freq_ids = 2 * position + jnp.arange(2, dtype=jnp.int32)
    cos_twist, sin_twist = angle_pair(freq_ids, jnp.arange(local_len), period)
    cos_twist = cos_twist[:, :, None]
    sin_twist = sin_twist[:, :, None]
    pieces = []
    for spec_pair in (first_spec, second_spec, third_spec):
        real_in, imag_in = spec_pair
        back_real = jnp.einsum(
            "rk,jkw->jrw", cos_local, real_in, precision=exact_mode
        ) - jnp.einsum("rk,jkw->jrw", sin_local, imag_in, precision=exact_mode)
        back_imag = jnp.einsum(
            "rk,jkw->jrw", cos_local, imag_in, precision=exact_mode
        ) + jnp.einsum("rk,jkw->jrw", sin_local, real_in, precision=exact_mode)
        pieces.append(back_real * cos_twist - back_imag * sin_twist)
        pieces.append(back_real * sin_twist + back_imag * cos_twist)
    gathered = (
        lax.all_to_all(pieces[0], "ctx", split_axis=1, concat_axis=0, tiled=True),
        lax.all_to_all(pieces[1], "ctx", split_axis=1, concat_axis=0, tiled=True),
        lax.all_to_all(pieces[2], "ctx", split_axis=1, concat_axis=0, tiled=True),
        lax.all_to_all(pieces[3], "ctx", split_axis=1, concat_axis=0, tiled=True),
        lax.all_to_all(pieces[4], "ctx", split_axis=1, concat_axis=0, tiled=True),
        lax.all_to_all(pieces[5], "ctx", split_axis=1, concat_axis=0, tiled=True),
    )
    cos_blocks, sin_blocks = angle_pair(jnp.arange(shards), jnp.arange(2 * shards), 2 * shards)
    outputs = []
    for member in range(3):
        real_in = gathered[2 * member]
        imag_in = gathered[2 * member + 1]
        channels = real_in.shape[2]
        values = jnp.dot(
            cos_blocks, real_in.reshape(2 * shards, stride * channels), precision=exact_mode
        ) - jnp.dot(
            sin_blocks, imag_in.reshape(2 * shards, stride * channels), precision=exact_mode
        )
        outputs.append((values / period).reshape(shards, stride, channels))
    returned = (
        lax.all_to_all(outputs[0], "ctx", split_axis=0, concat_axis=0, tiled=True),
        lax.all_to_all(outputs[1], "ctx", split_axis=0, concat_axis=0, tiled=True),
        lax.all_to_all(outputs[2], "ctx", split_axis=0, concat_axis=0, tiled=True),
    )
    return (
        returned[0].reshape(local_len, returned[0].shape[2]),
        returned[1].reshape(local_len, returned[1].shape[2]),
        returned[2].reshape(local_len, returned[2].shape[2]),
    )


def spectral_product(left_pair, right_pair):
    return (
        left_pair[0] * right_pair[0] - left_pair[1] * right_pair[1],
        left_pair[0] * right_pair[1] + left_pair[1] * right_pair[0],
    )


def conjugate_product(left_pair, right_pair):
    return (
        left_pair[0] * right_pair[0] + left_pair[1] * right_pair[1],
        left_pair[0] * right_pair[1] - left_pair[1] * right_pair[0],
    )


def on_device(query_gate, key_gate, value_gate, out_grad, filter_taps, skip):
    shards = lax.axis_size("ctx")
    query_vals = query_gate.astype(jnp.float32)
    key_vals = key_gate.astype(jnp.float32)
    value_vals = value_gate.astype(jnp.float32)
    grads = out_grad.astype(jnp.float32)
    gated = key_vals * value_vals
    grad_conv = grads * query_vals
    local_len = gated.shape[0]
    root_scale = 1.0 / math.sqrt(shards * local_len)
    gated_spec, conv_spec, filter_spec = forward_three(gated, grad_conv, filter_taps)
    conv_prod = spectral_product(filter_spec, gated_spec)
    back_prod = conjugate_product(filter_spec, conv_spec)
    corr_spec = conjugate_product(gated_spec, conv_spec)
    conv_time, back_time, corr_time = inverse_blocks(conv_prod, back_prod, corr_spec)
    conv_full = conv_time + skip[None, :] * gated
    grad_query = (grads * conv_full).astype(jnp.bfloat16)
    back_full = back_time + skip[None, :] * grad_conv
    grad_key = (back_full * value_vals).astype(jnp.bfloat16)
    grad_value = (back_full * key_vals).astype(jnp.bfloat16)
    grad_filter = corr_time * root_scale
    skip_term = jnp.sum(grad_conv * gated, axis=0) * root_scale
    grad_skip = lax.psum(skip_term, "ctx")
    return (grad_query, grad_key, grad_value, grad_filter, grad_skip)


def solution(mesh):
    return jax.shard_map(
        on_device,
        mesh=mesh,
        in_specs=(
            P("ctx", "dp"),
            P("ctx", "dp"),
            P("ctx", "dp"),
            P("ctx", "dp"),
            P("ctx", "dp"),
            P("dp"),
        ),
        out_specs=(P("ctx", "dp"), P("ctx", "dp"), P("ctx", "dp"), P("ctx", "dp"), P("dp")),
        check_vma=False,
    )
```

profile of v0, /device:TPU:6, one launch (start us, length us, event | category | flops | bytes accessed | tf_op | source)
XLA Modules:
  0.0 793.0 jit_solution(815683077738056679)
XLA Ops:
  2.8 14.8 %all-to-all-start.3 = ((f32[64,2,1024]{2,1,0:T(2,128)}), f32[64,2,1024]{2,1,0:T(2,128)S(1)}, u32[]{:S(2)}, u32[]{:S(2)}) async-start(f32[64,2,1024]{2,1,0:T(2,128)} %reshape.197), calls=%async_computation.3 | async-start | bytes 1048576 | tf_op jit(solution)/shard_map/all_to_all | solution.py:60
  18.8 15.1 %all-to-all-done.3 = f32[64,2,1024]{2,1,0:T(2,128)S(1)} async-done(((f32[64,2,1024]{2,1,0:T(2,128)}), f32[64,2,1024]{2,1,0:T(2,128)S(1)}, u32[]{:S(2)}, u32[]{:S(2)}) %all-to-all-start.3) | async-done | bytes 524320 | tf_op jit(solution)/shard_map/all_to_all | solution.py:60
  33.9 8.8 %all-to-all-start = ((f32[64,2,1024]{2,1,0:T(2,128)}), f32[64,2,1024]{2,1,0:T(2,128)S(1)}, u32[]{:S(2)}, u32[]{:S(2)}) async-start(f32[64,2,1024]{2,1,0:T(2,128)} %reshape.195), calls=%async_computation | async-start | bytes 1048576 | tf_op jit(solution)/shard_map/all_to_all | solution.py:66
  44.1 14.4 %all-to-all-done = f32[64,2,1024]{2,1,0:T(2,128)S(1)} async-done(((f32[64,2,1024]{2,1,0:T(2,128)}), f32[64,2,1024]{2,1,0:T(2,128)S(1)}, u32[]{:S(2)}, u32[]{:S(2)}) %all-to-all-start) | async-done | bytes 524320 | tf_op jit(solution)/shard_map/all_to_all | solution.py:66
  58.5 8.9 %all-to-all-start.9 = ((f32[64,2,1024]{2,1,0:T(2,128)}), f32[64,2,1024]{2,1,0:T(2,128)S(1)}, u32[]{:S(2)}, u32[]{:S(2)}) async-start(f32[64,2,1024]{2,1,0:T(2,128)} %reshape.203), calls=%async_computation.9 | async-start | bytes 1048576 | tf_op jit(solution)/shard_map/all_to_all | solution.py:63
  91.0 9.0 %all-to-all-start.1 = ((f32[128,2,1024]{2,1,0:T(2,128)}), f32[128,2,1024]{2,1,0:T(2,128)}, u32[]{:S(2)}, u32[]{:S(2)}) async-start(f32[128,2,1024]{2,1,0:T(2,128)} %copy.55), calls=%async_computation.1 | async-start | bytes 2097152 | tf_op jit(solution)/shard_map/all_to_all | solution.py:78
  101.9 23.7 %all-to-all-done.1 = f32[128,2,1024]{2,1,0:T(2,128)} async-done(((f32[128,2,1024]{2,1,0:T(2,128)}), f32[128,2,1024]{2,1,0:T(2,128)}, u32[]{:S(2)}, u32[]{:S(2)}) %all-to-all-start.1) | async-done | bytes 1048608 | tf_op jit(solution)/shard_map/all_to_all | solution.py:78
  125.6 9.4 %all-to-all-start.2 = ((f32[128,2,1024]{2,1,0:T(2,128)}), f32[128,2,1024]{2,1,0:T(2,128)}, u32[]{:S(2)}, u32[]{:S(2)}) async-start(f32[128,2,1024]{2,1,0:T(2,128)} %copy.58), calls=%async_computation.2 | async-start | bytes 2097152 | tf_op jit(solution)/shard_map/all_to_all | solution.py:79
  136.7 23.5 %all-to-all-done.2 = f32[128,2,1024]{2,1,0:T(2,128)} async-done(((f32[128,2,1024]{2,1,0:T(2,128)}), f32[128,2,1024]{2,1,0:T(2,128)}, u32[]{:S(2)}, u32[]{:S(2)}) %all-to-all-start.2) | async-done | bytes 1048608 | tf_op jit(solution)/shard_map/all_to_all | solution.py:79
  160.3 9.0 %all-to-all-start.10 = ((f32[128,2,1024]{2,1,0:T(2,128)}), f32[128,2,1024]{2,1,0:T(2,128)}, u32[]{:S(2)}, u32[]{:S(2)}) async-start(f32[128,2,1024]{2,1,0:T(2,128)} %copy.79), calls=%async_computation.10 | async-start | bytes 2097152 | tf_op jit(solution)/shard_map/all_to_all | solution.py:76
  171.1 23.7 %all-to-all-done.10 = f32[128,2,1024]{2,1,0:T(2,128)} async-done(((f32[128,2,1024]{2,1,0:T(2,128)}), f32[128,2,1024]{2,1,0:T(2,128)}, u32[]{:S(2)}, u32[]{:S(2)}) %all-to-all-start.10) | async-done | bytes 1048608 | tf_op jit(solution)/shard_map/all_to_all | solution.py:76
  194.8 8.8 %all-to-all-start.11 = ((f32[128,2,1024]{2,1,0:T(2,128)}), f32[128,2,1024]{2,1,0:T(2,128)S(1)}, u32[]{:S(2)}, u32[]{:S(2)}) async-start(f32[128,2,1024]{2,1,0:T(2,128)} %copy.82), calls=%async_computation.11 | async-start | bytes 2097152 | tf_op jit(solution)/shard_map/all_to_all | solution.py:77
  205.3 23.8 %all-to-all-done.11 = f32[128,2,1024]{2,1,0:T(2,128)S(1)} async-done(((f32[128,2,1024]{2,1,0:T(2,128)}), f32[128,2,1024]{2,1,0:T(2,128)S(1)}, u32[]{:S(2)}, u32[]{:S(2)}) %all-to-all-start.11) | async-done | bytes 1048608 | tf_op jit(solution)/shard_map/all_to_all | solution.py:77
  230.1 8.8 %all-to-all-start.4 = ((f32[128,2,1024]{2,1,0:T(2,128)}), f32[128,2,1024]{2,1,0:T(2,128)S(1)}, u32[]{:S(2)}, u32[]{:S(2)}) async-start(f32[128,2,1024]{2,1,0:T(2,128)} %copy.63), calls=%async_computation.4 | async-start | bytes 2097152 | tf_op jit(solution)/shard_map/all_to_all | solution.py:74
  243.2 21.4 %all-to-all-done.4 = f32[128,2,1024]{2,1,0:T(2,128)S(1)} async-done(((f32[128,2,1024]{2,1,0:T(2,128)}), f32[128,2,1024]{2,1,0:T(2,128)S(1)}, u32[]{:S(2)}, u32[]{:S(2)}) %all-to-all-start.4) | async-done | bytes 1048608 | tf_op jit(solution)/shard_map/all_to_all | solution.py:74
  264.5 9.0 %all-to-all-start.5 = ((f32[128,2,1024]{2,1,0:T(2,128)}), f32[128,2,1024]{2,1,0:T(2,128)}, u32[]{:S(2)}, u32[]{:S(2)}) async-start(f32[128,2,1024]{2,1,0:T(2,128)} %copy.66), calls=%async_computation.5 | async-start | bytes 2097152 | tf_op jit(solution)/shard_map/all_to_all | solution.py:75
  334.8 13.0 %all-to-all-start.15 = ((f32[2,128,1024]{2,0,1:T(2,128)}), f32[2,128,1024]{2,0,1:T(2,128)}, u32[]{:S(2)}, u32[]{:S(2)}) async-start(f32[2,128,1024]{2,0,1:T(2,128)} %copy.91), calls=%async_computation.15 | async-start | bytes 2097152 | tf_op jit(solution)/shard_map/all_to_all | solution.py:115
  350.0 22.7 %all-to-all-done.15 = f32[2,128,1024]{2,0,1:T(2,128)} async-done(((f32[2,128,1024]{2,0,1:T(2,128)}), f32[2,128,1024]{2,0,1:T(2,128)}, u32[]{:S(2)}, u32[]{:S(2)}) %all-to-all-start.15) | async-done | bytes 1048608 | tf_op jit(solution)/shard_map/all_to_all | solution.py:115
  372.7 9.5 %all-to-all-start.16 = ((f32[2,128,1024]{2,0,1:T(2,128)}), f32[2,128,1024]{2,0,1:T(2,128)}, u32[]{:S(2)}, u32[]{:S(2)}) async-start(f32[2,128,1024]{2,0,1:T(2,128)} %copy.93), calls=%async_computation.16 | async-start | bytes 2097152 | tf_op jit(solution)/shard_map/all_to_all | solution.py:116
  384.6 22.4 %all-to-all-done.16 = f32[2,128,1024]{2,0,1:T(2,128)} async-done(((f32[2,128,1024]{2,0,1:T(2,128)}), f32[2,128,1024]{2,0,1:T(2,128)}, u32[]{:S(2)}, u32[]{:S(2)}) %all-to-all-start.16) | async-done | bytes 1048608 | tf_op jit(solution)/shard_map/all_to_all | solution.py:116
  407.0 9.0 %all-to-all-start.6 = ((f32[2,128,1024]{2,0,1:T(2,128)}), f32[2,128,1024]{2,0,1:T(2,128)}, u32[]{:S(2)}, u32[]{:S(2)}) async-start(f32[2,128,1024]{2,0,1:T(2,128)} %copy.73), calls=%async_computation.6 | async-start | bytes 2097152 | tf_op jit(solution)/shard_map/all_to_all | solution.py:111
  417.3 23.6 %all-to-all-done.6 = f32[2,128,1024]{2,0,1:T(2,128)} async-done(((f32[2,128,1024]{2,0,1:T(2,128)}), f32[2,128,1024]{2,0,1:T(2,128)}, u32[]{:S(2)}, u32[]{:S(2)}) %all-to-all-start.6) | async-done | bytes 1048608 | tf_op jit(solution)/shard_map/all_to_all | solution.py:111
  440.9 8.8 %all-to-all-start.7 = ((f32[2,128,1024]{2,0,1:T(2,128)}), f32[2,128,1024]{2,0,1:T(2,128)S(1)}, u32[]{:S(2)}, u32[]{:S(2)}) async-start(f32[2,128,1024]{2,0,1:T(2,128)} %copy.75), calls=%async_computation.7 | async-start | bytes 2097152 | tf_op jit(solution)/shard_map/all_to_all | solution.py:112
  451.0 23.6 %all-to-all-done.7 = f32[2,128,1024]{2,0,1:T(2,128)S(1)} async-done(((f32[2,128,1024]{2,0,1:T(2,128)}), f32[2,128,1024]{2,0,1:T(2,128)S(1)}, u32[]{:S(2)}, u32[]{:S(2)}) %all-to-all-start.7) | async-done | bytes 1048608 | tf_op jit(solution)/shard_map/all_to_all | solution.py:112
  474.6 8.8 %all-to-all-start.12 = ((f32[2,128,1024]{2,0,1:T(2,128)}), f32[2,128,1024]{2,0,1:T(2,128)S(1)}, u32[]{:S(2)}, u32[]{:S(2)}) async-start(f32[2,128,1024]{2,0,1:T(2,128)} %copy.87), calls=%async_computation.12 | async-start | bytes 2097152 | tf_op jit(solution)/shard_map/all_to_all | solution.py:113
  484.7 23.6 %all-to-all-done.12 = f32[2,128,1024]{2,0,1:T(2,128)S(1)} async-done(((f32[2,128,1024]{2,0,1:T(2,128)}), f32[2,128,1024]{2,0,1:T(2,128)S(1)}, u32[]{:S(2)}, u32[]{:S(2)}) %all-to-all-start.12) | async-done | bytes 1048608 | tf_op jit(solution)/shard_map/all_to_all | solution.py:113
  508.3 8.8 %all-to-all-start.13 = ((f32[2,128,1024]{2,0,1:T(2,128)}), f32[2,128,1024]{2,0,1:T(2,128)S(1)}, u32[]{:S(2)}, u32[]{:S(2)}) async-start(f32[2,128,1024]{2,0,1:T(2,128)} %copy.89), calls=%async_computation.13 | async-start | bytes 2097152 | tf_op jit(solution)/shard_map/all_to_all | solution.py:114
  526.0 16.0 %all-to-all-done.13 = f32[2,128,1024]{2,0,1:T(2,128)S(1)} async-done(((f32[2,128,1024]{2,0,1:T(2,128)}), f32[2,128,1024]{2,0,1:T(2,128)S(1)}, u32[]{:S(2)}, u32[]{:S(2)}) %all-to-all-start.13) | async-done | bytes 1048608 | tf_op jit(solution)/shard_map/all_to_all | solution.py:114
  542.0 9.3 %all-to-all-start.17 = ((f32[64,2,1024]{2,1,0:T(2,128)}), f32[64,2,1024]{2,1,0:T(2,128)}, u32[]{:S(2)}, u32[]{:S(2)}) async-start(f32[64,2,1024]{2,1,0:T(2,128)} %reshape.211), calls=%async_computation.17 | async-start | bytes 1048576 | tf_op jit(solution)/shard_map/all_to_all | solution.py:133
  587.1 8.8 %all-to-all-start.14 = ((f32[64,2,1024]{2,1,0:T(2,128)}), f32[64,2,1024]{2,1,0:T(2,128)S(1)}, u32[]{:S(2)}, u32[]{:S(2)}) async-start(f32[64,2,1024]{2,1,0:T(2,128)} %reshape.207), calls=%async_computation.14 | async-start | bytes 1048576 | tf_op jit(solution)/shard_map/all_to_all | solution.py:132
  598.7 10.5 %all-to-all-done.14 = f32[64,2,1024]{2,1,0:T(2,128)S(1)} async-done(((f32[64,2,1024]{2,1,0:T(2,128)}), f32[64,2,1024]{2,1,0:T(2,128)S(1)}, u32[]{:S(2)}, u32[]{:S(2)}) %all-to-all-start.14) | async-done | bytes 524320 | tf_op jit(solution)/shard_map/all_to_all | solution.py:132
  610.9 182.0 %psum.7 = f32[1024]{0:T(1024)} all-reduce(f32[1024]{0:T(1024)S(1)} %broadcast_multiply_fusion.1), channel_id=1, replica_groups=mesh['dp'=4,'ctx'=64] {'ctx'}, use_global_device_ids=true, to_apply=%region_1.2 | all-reduce | flops 1024 | bytes 8192 | tf_op jit(solution)/shard_map/psum | solution.py:178
  (138 shorter events, 159.1 us)
Async XLA Ops:
  2.8 14.9 %copy-start.20 = (f32[128,1024]{1,0:T(8,128)S(1)}, f32[128,1024]{1,0:T(8,128)}, u32[]{:S(2)}) copy-start(f32[128,1024]{1,0:T(8,128)} %param.10) | copy-start | bytes 1572868
  2.8 31.1 %all-to-all-start.3 = ((f32[64,2,1024]{2,1,0:T(2,128)}), f32[64,2,1024]{2,1,0:T(2,128)S(1)}, u32[]{:S(2)}, u32[]{:S(2)}) async-start(f32[64,2,1024]{2,1,0:T(2,128)} %reshape.197), calls=%async_computation.3 | async-start | bytes 1048576 | tf_op jit(solution)/shard_map/all_to_all | solution.py:60
  18.8 24.0 %copy-start.16 = (bf16[128,1024]{1,0:T(8,128)(2,1)S(1)}, bf16[128,1024]{1,0:T(8,128)(2,1)}, u32[]{:S(2)}) copy-start(bf16[128,1024]{1,0:T(8,128)(2,1)} %param.9) | copy-start | bytes 786436
  18.8 24.0 %copy-start.17 = (bf16[128,1024]{1,0:T(8,128)(2,1)S(1)}, bf16[128,1024]{1,0:T(8,128)(2,1)}, u32[]{:S(2)}) copy-start(bf16[128,1024]{1,0:T(8,128)(2,1)} %param.6) | copy-start | bytes 786436
  33.9 24.6 %all-to-all-start = ((f32[64,2,1024]{2,1,0:T(2,128)}), f32[64,2,1024]{2,1,0:T(2,128)S(1)}, u32[]{:S(2)}, u32[]{:S(2)}) async-start(f32[64,2,1024]{2,1,0:T(2,128)} %reshape.195), calls=%async_computation | async-start | bytes 1048576 | tf_op jit(solution)/shard_map/all_to_all | solution.py:66
  58.5 24.0 %all-to-all-start.9 = ((f32[64,2,1024]{2,1,0:T(2,128)}), f32[64,2,1024]{2,1,0:T(2,128)S(1)}, u32[]{:S(2)}, u32[]{:S(2)}) async-start(f32[64,2,1024]{2,1,0:T(2,128)} %reshape.203), calls=%async_computation.9 | async-start | bytes 1048576 | tf_op jit(solution)/shard_map/all_to_all | solution.py:63
  91.0 9.0 %copy-start.7 = (f32[128,2,1024]{2,0,1:T(8,128)S(1)}, f32[128,2,1024]{2,0,1:T(8,128)}, u32[]{:S(2)}) copy-start(f32[128,2,1024]{2,0,1:T(8,128)} %get-tuple-element.37) | copy-start | bytes 3145732
  91.0 34.5 %all-to-all-start.1 = ((f32[128,2,1024]{2,1,0:T(2,128)}), f32[128,2,1024]{2,1,0:T(2,128)}, u32[]{:S(2)}, u32[]{:S(2)}) async-start(f32[128,2,1024]{2,1,0:T(2,128)} %copy.55), calls=%async_computation.1 | async-start | bytes 2097152 | tf_op jit(solution)/shard_map/all_to_all | solution.py:78
  101.9 33.1 %copy-start.4 = (f32[128,2,1024]{2,0,1:T(8,128)S(1)}, f32[128,2,1024]{2,0,1:T(8,128)}, u32[]{:S(2)}) copy-start(f32[128,2,1024]{2,0,1:T(8,128)} %get-tuple-element.16) | copy-start | bytes 3145732
  125.6 34.7 %all-to-all-start.2 = ((f32[128,2,1024]{2,1,0:T(2,128)}), f32[128,2,1024]{2,1,0:T(2,128)}, u32[]{:S(2)}, u32[]{:S(2)}) async-start(f32[128,2,1024]{2,1,0:T(2,128)} %copy.58), calls=%async_computation.2 | async-start | bytes 2097152 | tf_op jit(solution)/shard_map/all_to_all | solution.py:79
  136.7 32.5 %copy-start.3 = (f32[128,2,1024]{2,0,1:T(8,128)S(1)}, f32[128,2,1024]{2,0,1:T(8,128)}, u32[]{:S(2)}) copy-start(f32[128,2,1024]{2,0,1:T(8,128)} %get-tuple-element.15) | copy-start | bytes 3145732
  160.3 34.5 %all-to-all-start.10 = ((f32[128,2,1024]{2,1,0:T(2,128)}), f32[128,2,1024]{2,1,0:T(2,128)}, u32[]{:S(2)}, u32[]{:S(2)}) async-start(f32[128,2,1024]{2,1,0:T(2,128)} %copy.79), calls=%async_computation.10 | async-start | bytes 2097152 | tf_op jit(solution)/shard_map/all_to_all | solution.py:76
  194.8 34.4 %all-to-all-start.11 = ((f32[128,2,1024]{2,1,0:T(2,128)}), f32[128,2,1024]{2,1,0:T(2,128)S(1)}, u32[]{:S(2)}, u32[]{:S(2)}) async-start(f32[128,2,1024]{2,1,0:T(2,128)} %copy.82), calls=%async_computation.11 | async-start | bytes 2097152 | tf_op jit(solution)/shard_map/all_to_all | solution.py:77
  230.1 34.4 %all-to-all-start.4 = ((f32[128,2,1024]{2,1,0:T(2,128)}), f32[128,2,1024]{2,1,0:T(2,128)S(1)}, u32[]{:S(2)}, u32[]{:S(2)}) async-start(f32[128,2,1024]{2,1,0:T(2,128)} %copy.63), calls=%async_computation.4 | async-start | bytes 2097152 | tf_op jit(solution)/shard_map/all_to_all | solution.py:74
  264.5 11.2 %copy-start.11 = (f32[128,2,1024]{2,1,0:T(2,128)}, f32[128,2,1024]{2,1,0:T(2,128)S(1)}, u32[]{:S(2)}) copy-start(f32[128,2,1024]{2,1,0:T(2,128)S(1)} %all-to-all-done.4) | copy-start | bytes 3145732
  264.5 41.7 %all-to-all-start.5 = ((f32[128,2,1024]{2,1,0:T(2,128)}), f32[128,2,1024]{2,1,0:T(2,128)}, u32[]{:S(2)}, u32[]{:S(2)}) async-start(f32[128,2,1024]{2,1,0:T(2,128)} %copy.66), calls=%async_computation.5 | async-start | bytes 2097152 | tf_op jit(solution)/shard_map/all_to_all | solution.py:75
  295.1 2.2 copy-start
  297.3 2.2 copy-start.8
  309.9 2.5 copy-start.14
  334.8 38.0 %all-to-all-start.15 = ((f32[2,128,1024]{2,0,1:T(2,128)}), f32[2,128,1024]{2,0,1:T(2,128)}, u32[]{:S(2)}, u32[]{:S(2)}) async-start(f32[2,128,1024]{2,0,1:T(2,128)} %copy.91), calls=%async_computation.15 | async-start | bytes 2097152 | tf_op jit(solution)/shard_map/all_to_all | solution.py:115
  372.7 34.3 %all-to-all-start.16 = ((f32[2,128,1024]{2,0,1:T(2,128)}), f32[2,128,1024]{2,0,1:T(2,128)}, u32[]{:S(2)}, u32[]{:S(2)}) async-start(f32[2,128,1024]{2,0,1:T(2,128)} %copy.93), calls=%async_computation.16 | async-start | bytes 2097152 | tf_op jit(solution)/shard_map/all_to_all | solution.py:116
  407.0 33.9 %all-to-all-start.6 = ((f32[2,128,1024]{2,0,1:T(2,128)}), f32[2,128,1024]{2,0,1:T(2,128)}, u32[]{:S(2)}, u32[]{:S(2)}) async-start(f32[2,128,1024]{2,0,1:T(2,128)} %copy.73), calls=%async_computation.6 | async-start | bytes 2097152 | tf_op jit(solution)/shard_map/all_to_all | solution.py:111
  440.9 33.7 %all-to-all-start.7 = ((f32[2,128,1024]{2,0,1:T(2,128)}), f32[2,128,1024]{2,0,1:T(2,128)S(1)}, u32[]{:S(2)}, u32[]{:S(2)}) async-start(f32[2,128,1024]{2,0,1:T(2,128)} %copy.75), calls=%async_computation.7 | async-start | bytes 2097152 | tf_op jit(solution)/shard_map/all_to_all | solution.py:112
  474.6 33.7 %all-to-all-start.12 = ((f32[2,128,1024]{2,0,1:T(2,128)}), f32[2,128,1024]{2,0,1:T(2,128)S(1)}, u32[]{:S(2)}, u32[]{:S(2)}) async-start(f32[2,128,1024]{2,0,1:T(2,128)} %copy.87), calls=%async_computation.12 | async-start | bytes 2097152 | tf_op jit(solution)/shard_map/all_to_all | solution.py:113
  508.3 33.7 %all-to-all-start.13 = ((f32[2,128,1024]{2,0,1:T(2,128)}), f32[2,128,1024]{2,0,1:T(2,128)S(1)}, u32[]{:S(2)}, u32[]{:S(2)}) async-start(f32[2,128,1024]{2,0,1:T(2,128)} %copy.89), calls=%async_computation.13 | async-start | bytes 2097152 | tf_op jit(solution)/shard_map/all_to_all | solution.py:114
  542.0 22.9 %all-to-all-start.17 = ((f32[64,2,1024]{2,1,0:T(2,128)}), f32[64,2,1024]{2,1,0:T(2,128)}, u32[]{:S(2)}, u32[]{:S(2)}) async-start(f32[64,2,1024]{2,1,0:T(2,128)} %reshape.211), calls=%async_computation.17 | async-start | bytes 1048576 | tf_op jit(solution)/shard_map/all_to_all | solution.py:133
  565.0 22.1 %all-to-all-start.8 = ((f32[64,2,1024]{2,1,0:T(2,128)}), f32[64,2,1024]{2,1,0:T(2,128)S(1)}, u32[]{:S(2)}, u32[]{:S(2)}) async-start(f32[64,2,1024]{2,1,0:T(2,128)} %reshape.201), calls=%async_computation.8 | async-start | bytes 1048576 | tf_op jit(solution)/shard_map/all_to_all | solution.py:131
  587.1 22.1 %all-to-all-start.14 = ((f32[64,2,1024]{2,1,0:T(2,128)}), f32[64,2,1024]{2,1,0:T(2,128)S(1)}, u32[]{:S(2)}, u32[]{:S(2)}) async-start(f32[64,2,1024]{2,1,0:T(2,128)} %reshape.207), calls=%async_computation.14 | async-start | bytes 1048576 | tf_op jit(solution)/shard_map/all_to_all | solution.py:132
  598.7 10.9 %copy-start.15 = (bf16[128,1024]{1,0:T(8,128)(2,1)S(1)}, bf16[128,1024]{1,0:T(8,128)(2,1)}, u32[]{:S(2)}) copy-start(bf16[128,1024]{1,0:T(8,128)(2,1)} %param.7) | copy-start | bytes 786436
  598.7 10.9 %copy-start.18 = (bf16[128,1024]{1,0:T(8,128)(2,1)S(1)}, bf16[128,1024]{1,0:T(8,128)(2,1)}, u32[]{:S(2)}) copy-start(bf16[128,1024]{1,0:T(8,128)(2,1)} %param.6) | copy-start | bytes 786436
  598.7 10.9 %copy-start.19 = (bf16[128,1024]{1,0:T(8,128)(2,1)S(1)}, bf16[128,1024]{1,0:T(8,128)(2,1)}, u32[]{:S(2)}) copy-start(bf16[128,1024]{1,0:T(8,128)(2,1)} %param.8) | copy-start | bytes 786436
  598.7 10.9 %copy-start.21 = (f32[1024]{0:T(1024)S(1)}, f32[1024]{0:T(1024)}, u32[]{:S(2)}) copy-start(f32[1024]{0:T(1024)} %param.11) | copy-start | bytes 12292
  (8 other events, 10.8 us)
where the time goes:
time: 799 us; the launch traced here: 793 us
  waiting for transfers between devices  311 us (39%)
  blocking collectives  182 us (23%)
  starting transfers between devices  171 us (21%)
  local copies, waits for them, and re-layouts  64 us (8%)
  matrix products  59.6 us (7%)
    psum x1, blocking collectives, on_device(): grad_skip = lax.psum(skip_term, 'ctx')  182 us
    all_to_all x1, waiting for transfers between devices, forward_three(): lax.all_to_all(second_tw[1], 'ctx', split_axis=0, concat_axis=1, tiled=True)  23.8 us
    all_to_all x1, waiting for transfers between devices, forward_three(): lax.all_to_all(third_tw[0], 'ctx', split_axis=0, concat_axis=1, tiled=True)  23.7 us
    all_to_all x1, waiting for transfers between devices, forward_three(): lax.all_to_all(second_tw[0], 'ctx', split_axis=0, concat_axis=1, tiled=True)  23.7 us
    all_to_all x1, waiting for transfers between devices, inverse_blocks(): lax.all_to_all(pieces[2], 'ctx', split_axis=1, concat_axis=0, tiled=True)  23.6 us
    all_to_all x1, waiting for transfers between devices, inverse_blocks(): lax.all_to_all(pieces[1], 'ctx', split_axis=1, concat_axis=0, tiled=True)  23.6 us
    all_to_all x1, waiting for transfers between devices, inverse_blocks(): lax.all_to_all(pieces[0], 'ctx', split_axis=1, concat_axis=0, tiled=True)  23.6 us
    all_to_all x1, waiting for transfers between devices, forward_three(): lax.all_to_all(third_tw[1], 'ctx', split_axis=0, concat_axis=1, tiled=True)  23.5 us
  transfers between devices with their start and end apart: 18, of which 17 were waited for; matrix products, arithmetic and copies ran while one was open for 11% of the time, Pallas kernels for 0%

commit v1 on v0

v1 whole, which is shorter than its diff:
```python
import functools
import math

import jax
import jax.numpy as jnp
import ml_dtypes
import numpy as np
from jax import lax
from jax.experimental import pallas as pl
from jax.experimental.pallas import tpu as pltpu
from jax.sharding import PartitionSpec as P

MESH = pl.DeviceIdType.MESH
BLOCKS = 64
LANES = 128
WIDTH = 1024
OWN = WIDTH // BLOCKS
PERIOD = 2 * BLOCKS * LANES
HALF = 72
GROUP = 4
ROWS = GROUP * HALF
Z_ORDER = (1, 7, 3, 5, 2, 6, 4, 0)


def split_bf16(values):
    high = values.astype(ml_dtypes.bfloat16)
    low = (values - high.astype(np.float64)).astype(ml_dtypes.bfloat16)
    return high, low


@functools.cache
def tables():
    k1 = np.arange(HALF)[:, None]
    valid = (k1 <= BLOCKS).astype(np.float64)
    block = np.arange(BLOCKS)[None, :]
    angle = 2 * np.pi * ((k1 * block) % (2 * BLOCKS)) / (2 * BLOCKS)
    fwd_block = np.concatenate([np.cos(angle) * valid, -np.sin(angle) * valid])
    high, low = split_bf16(fwd_block)
    fwd_block = np.concatenate([high, high, low, low], axis=1)
    weight = np.where((k1 == 0) | (k1 == BLOCKS), 1.0, 2.0) * valid / PERIOD
    inv_block = np.concatenate([np.cos(angle) * weight, -np.sin(angle) * weight]).T
    inv_high, inv_low = split_bf16(inv_block)
    pad = np.zeros((BLOCKS, 256 - 2 * HALF), ml_dtypes.bfloat16)
    inv_block = np.concatenate(
        [np.concatenate([inv_high, pad], 1), np.concatenate([inv_low, pad], 1)]
    )
    ids = np.arange(LANES)
    local = 2 * np.pi * ((ids[:, None] * ids[None, :]) % LANES) / LANES
    cos, sin = np.cos(local), np.sin(local)
    fwd_local = np.block([[cos, -sin], [sin, cos]])
    inv_local = np.block([[cos, sin], [-sin, cos]])
    matrices = np.concatenate([fwd_block, *split_bf16(fwd_local), *split_bf16(inv_local), inv_block])
    twist = 2 * np.pi * ((k1 * ids[None, :]) % PERIOD) / PERIOD
    twists = np.concatenate([np.cos(twist), np.sin(twist)]).astype(np.float32)
    return matrices, twists


FWD_BLOCK = 0
FWD_HIGH = 2 * HALF
FWD_LOW = FWD_HIGH + 256
INV_HIGH = FWD_LOW + 256
INV_LOW = INV_HIGH + 256
INV_BLOCK = INV_LOW + 256


def halves(values):
    high = values.astype(jnp.bfloat16)
    return high, (values - high.astype(jnp.float32)).astype(jnp.bfloat16)


def dot(left, right):
    return jnp.dot(left, right, preferred_element_type=jnp.float32)


def kernel(
    query_hbm, key_hbm, value_hbm, grads_hbm, taps_hbm, skip_hbm, mats_hbm, twists_hbm,
    gq_hbm, gk_hbm, gv_hbm, gf_hbm, gs_hbm,
    query, key, value, grads, taps, skip, mats, twists,
    gq, gk, gv, gf, gs,
    leaving, landed, spectra, rows_out, rows_in,
    load_sems, store_sems, send_sems, recv_sems,
):
    me = lax.axis_index("ctx")
    dp = lax.axis_index("dp")
    my_x, my_z, my_y = me // 32, (me // 4) % 8, me % 4

    loads = [
        pltpu.make_async_copy(src, dst, load_sems.at[i])
        for i, (src, dst) in enumerate(
            ((taps_hbm, taps), (key_hbm, key), (value_hbm, value), (grads_hbm, grads),
             (query_hbm, query), (twists_hbm, twists), (mats_hbm, mats), (skip_hbm, skip))
        )
    ]
    for load in loads:
        load.start()

    barrier = pltpu.get_barrier_semaphore()

    def greet(i, carry):
        there = lax.rem(me + 1 + i, BLOCKS)
        pl.semaphore_signal(barrier, inc=1, device_id=(dp, there), device_id_type=MESH)
        return carry

    lax.fori_loop(0, BLOCKS - 1, greet, 0)

    def rows_of(device):
        return pl.ds(pl.multiple_of(device * OWN, OWN), OWN)

    def to_all(send_one):
        def body(j, carry):
            for zi, dz in enumerate(Z_ORDER):
                xy = (j + zi) % 8 if dz else j
                there = ((my_x + xy // 4) % 2) * 32 + ((my_z + dz) % 8) * 4 + (my_y + xy) % 4
                if dz:
                    send_one(there)
                else:
                    @pl.when(j > 0)
                    def _():
                        send_one(there)
            return carry

        lax.fori_loop(0, 8, body, 0)

    def send_signal(s):
        def one(there):
            pltpu.make_async_remote_copy(
                src_ref=leaving.at[s, rows_of(there), :],
                dst_ref=landed.at[s, rows_of(me), :],
                send_sem=send_sems.at[s],
                recv_sem=recv_sems.at[s],
                device_id=(dp, there),
                device_id_type=MESH,
            ).start()

        to_all(one)
        landed[s, rows_of(me), :] = leaving[s, rows_of(me), :]

    def wait_bytes(s, sems):
        most = pl.ds(0, (BLOCKS - 1) * OWN)
        pltpu.make_async_copy(leaving.at[s, most, :], landed.at[s, most, :], sems.at[s]).wait()

    def columns(j):
        return slice(j * LANES, (j + 1) * LANES)

    loads[0].wait()
    for j in range(WIDTH // LANES):
        leaving[0, columns(j), :] = taps[:, columns(j)].T
    pl.semaphore_wait(barrier, BLOCKS - 1)
    send_signal(0)

    loads[1].wait()
    loads[2].wait()
    for j in range(WIDTH // LANES):
        gated = key[:, columns(j)].astype(jnp.float32) * value[:, columns(j)].astype(jnp.float32)
        leaving[1, columns(j), :] = gated.T
    send_signal(1)

    loads[3].wait()
    loads[4].wait()
    for j in range(WIDTH // LANES):
        conv_grad = grads[:, columns(j)].astype(jnp.float32) * query[:, columns(j)].astype(jnp.float32)
        leaving[2, columns(j), :] = conv_grad.T
    send_signal(2)

    for load in loads[5:]:
        load.wait()

    def forward(s):
        signal = landed.at[s]
        cos_twist, sin_twist = twists[0:HALF, :], twists[HALF:, :]
        for group in range(OWN // GROUP):
            lines = []
            for pair in range(GROUP // 2):
                first = group * GROUP + 2 * pair
                both = jnp.concatenate(
                    [signal[pl.ds(first + i, BLOCKS, stride=OWN), :] for i in range(2)], axis=1
                )
                high, low = halves(both)
                stacked = jnp.concatenate([high, low, high, low], axis=0)
                parts = dot(mats[FWD_BLOCK : FWD_BLOCK + 2 * HALF, :], stacked)
                for i in range(2):
                    real, imag = parts[:HALF, columns(i)], parts[HALF:, columns(i)]
                    lines.append(
                        jnp.concatenate(
                            [real * cos_twist + imag * sin_twist, imag * cos_twist - real * sin_twist],
                            axis=1,
                        )
                    )
            high, low = halves(jnp.concatenate(lines, axis=0))
            spectra[s, group * ROWS : (group + 1) * ROWS, :] = (
                dot(high, mats[FWD_HIGH : FWD_HIGH + 256, :])
                + dot(low, mats[FWD_HIGH : FWD_HIGH + 256, :])
                + dot(high, mats[FWD_LOW : FWD_LOW + 256, :])
            )

    def inverse(s, left, right, conjugate):
        result = leaving.at[3 + s]
        cos_twist, sin_twist = twists[0:HALF, :], twists[HALF:, :]
        for group in range(OWN // GROUP):
            rows = slice(group * ROWS, (group + 1) * ROWS)
            a_re, a_im = spectra[left, rows, 0:LANES], spectra[left, rows, LANES:]
            b_re, b_im = spectra[right, rows, 0:LANES], spectra[right, rows, LANES:]
            if conjugate:
                product = [a_re * b_re + a_im * b_im, a_re * b_im - a_im * b_re]
            else:
                product = [a_re * b_re - a_im * b_im, a_re * b_im + a_im * b_re]
            high, low = halves(jnp.concatenate(product, axis=1))
            back = (
                dot(high, mats[INV_HIGH : INV_HIGH + 256, :])
                + dot(low, mats[INV_HIGH : INV_HIGH + 256, :])
                + dot(high, mats[INV_LOW : INV_LOW + 256, :])
            )
            for pair in range(GROUP // 2):
                pieces = []
                for i in range(2):
                    top = (2 * pair + i) * HALF
                    real, imag = back[top : top + HALF, 0:LANES], back[top : top + HALF, LANES:]
                    pieces.append(
                        jnp.concatenate(
                            [real * cos_twist - imag * sin_twist, real * sin_twist + imag * cos_twist],
                            axis=0,
                        )
                    )
                high, low = halves(jnp.concatenate(pieces, axis=1))
                inv_high = mats[INV_BLOCK : INV_BLOCK + BLOCKS, 0 : 2 * HALF]
                inv_low = mats[INV_BLOCK + BLOCKS : INV_BLOCK + 2 * BLOCKS, 0 : 2 * HALF]
                values = dot(inv_high, high) + dot(inv_high, low) + dot(inv_low, high)
                first = group * GROUP + 2 * pair
                for i in range(2):
                    result[pl.ds(first + i, BLOCKS, stride=OWN), :] = values[:, columns(i)]

    wait_bytes(0, recv_sems)
    forward(0)
    wait_bytes(1, recv_sems)
    forward(1)
    inverse(0, 0, 1, False)
    send_signal(3)
    wait_bytes(2, recv_sems)
    forward(2)
    inverse(1, 0, 2, True)
    send_signal(4)
    inverse(2, 1, 2, True)
    send_signal(5)

    total = jnp.zeros((OWN, LANES), jnp.float32)
    for b in range(BLOCKS):
        total = total + landed[1, b * OWN : (b + 1) * OWN, :] * landed[2, b * OWN : (b + 1) * OWN, :]
    total = jnp.sum(total, axis=1, keepdims=True)
    lane = lax.broadcasted_iota(jnp.int32, (OWN, LANES), 1)
    channel = lax.broadcasted_iota(jnp.int32, (OWN, LANES), 0)
    placed = jnp.where(lane == channel + (me % 8) * OWN, total, 0.0)
    root_scale = 1.0 / math.sqrt(BLOCKS * LANES)
    rows_out[...] = jnp.sum(placed, axis=0, keepdims=True) * root_scale
    rows_in[pl.ds(me, 1)] = rows_out[...].reshape(1, 1, LANES)

    def send_row(there):
        pltpu.make_async_remote_copy(
            src_ref=rows_out,
            dst_ref=rows_in.at[me],
            send_sem=send_sems.at[6],
            recv_sem=recv_sems.at[6],
            device_id=(dp, there),
            device_id_type=MESH,
        ).start()

    to_all(send_row)

    wait_bytes(3, recv_sems)
    for j in range(WIDTH // LANES):
        gated = key[:, columns(j)].astype(jnp.float32) * value[:, columns(j)].astype(jnp.float32)
        conv = landed[3, columns(j), :].T + skip[:, columns(j)] * gated
        gq[:, columns(j)] = (grads[:, columns(j)].astype(jnp.float32) * conv).astype(jnp.bfloat16)
    stores = [pltpu.make_async_copy(gq, gq_hbm, store_sems.at[0])]
    stores[0].start()

    wait_bytes(4, recv_sems)
    for j in range(WIDTH // LANES):
        conv_grad = grads[:, columns(j)].astype(jnp.float32) * query[:, columns(j)].astype(jnp.float32)
        back = landed[4, columns(j), :].T + skip[:, columns(j)] * conv_grad
        gk[:, columns(j)] = (back * value[:, columns(j)].astype(jnp.float32)).astype(jnp.bfloat16)
        gv[:, columns(j)] = (back * key[:, columns(j)].astype(jnp.float32)).astype(jnp.bfloat16)
    for i, (src, dst) in enumerate(((gk, gk_hbm), (gv, gv_hbm))):
        stores.append(pltpu.make_async_copy(src, dst, store_sems.at[1 + i]))
        stores[-1].start()

    wait_bytes(5, recv_sems)
    for j in range(WIDTH // LANES):
        gf[:, columns(j)] = landed[5, columns(j), :].T * root_scale
    stores.append(pltpu.make_async_copy(gf, gf_hbm, store_sems.at[3]))
    stores[-1].start()

    most = pl.ds(0, BLOCKS - 1)
    pltpu.make_async_copy(rows_in.at[most], rows_in.at[most], recv_sems.at[6]).wait()
    gs[...] = jnp.sum(rows_in[...].reshape(8, 8, LANES), axis=1)
    stores.append(pltpu.make_async_copy(gs, gs_hbm, store_sems.at[4]))
    stores[-1].start()

    for s in range(6):
        wait_bytes(s, send_sems)
    pltpu.make_async_copy(rows_in.at[most], rows_in.at[most], send_sems.at[6]).wait()
    for store in stores:
        store.wait()


def on_device(query_gate, key_gate, value_gate, out_grad, filter_taps, skip):
    matrices, twists = tables()
    shape = query_gate.shape
    assert shape == (LANES, WIDTH) and lax.axis_size("ctx") == BLOCKS
    bf16, f32 = jnp.bfloat16, jnp.float32
    outs = pl.pallas_call(
        kernel,
        out_shape=[
            jax.ShapeDtypeStruct(shape, bf16),
            jax.ShapeDtypeStruct(shape, bf16),
            jax.ShapeDtypeStruct(shape, bf16),
            jax.ShapeDtypeStruct(shape, f32),
            jax.ShapeDtypeStruct((8, LANES), f32),
        ],
        in_specs=[pl.BlockSpec(memory_space=pl.ANY)] * 8,
        out_specs=[pl.BlockSpec(memory_space=pl.ANY)] * 5,
        scratch_shapes=[
            *[pltpu.VMEM(shape, bf16)] * 4,
            pltpu.VMEM(shape, f32),
            pltpu.VMEM((1, WIDTH), f32),
            pltpu.VMEM(matrices.shape, bf16),
            pltpu.VMEM(twists.shape, f32),
            *[pltpu.VMEM(shape, bf16)] * 3,
            pltpu.VMEM(shape, f32),
            pltpu.VMEM((8, LANES), f32),
            pltpu.VMEM((6, WIDTH, LANES), f32),
            pltpu.VMEM((6, WIDTH, LANES), f32),
            pltpu.VMEM((3, OWN * HALF, 2 * LANES), f32),
            pltpu.VMEM((1, LANES), f32),
            pltpu.VMEM((BLOCKS, 1, LANES), f32),
            pltpu.SemaphoreType.DMA((8,)),
            pltpu.SemaphoreType.DMA((5,)),
            pltpu.SemaphoreType.DMA((7,)),
            pltpu.SemaphoreType.DMA((7,)),
        ],
        compiler_params=pltpu.CompilerParams(
            collective_id=0, has_side_effects=True, vmem_limit_bytes=48 << 20
        ),
        cost_estimate=pl.CostEstimate(
            flops=4 * 10**9, bytes_accessed=3 * 10**6, transcendentals=0
        ),
        name="hyena_backward",
    )(
        query_gate, key_gate, value_gate, out_grad, filter_taps, skip.reshape(1, WIDTH),
        jnp.asarray(matrices), jnp.asarray(twists),
    )
    return (*outs[:4], outs[4].reshape(WIDTH))


def solution(mesh):
    return jax.shard_map(
        on_device,
        mesh=mesh,
        in_specs=(*[P("ctx", "dp")] * 5, P("dp")),
        out_specs=(*[P("ctx", "dp")] * 4, P("dp")),
        check_vma=False,
    )
```

time: 799 us -> 96.1 us (0.12)
  waiting for transfers between devices: 311 us -> 0 us
  blocking collectives: 182 us -> 0 us
  starting transfers between devices: 171 us -> 0 us
  Pallas kernels: 0 us -> 84.1 us
  matrix products: 59.6 us -> 0 us
  local copies, waits for them, and re-layouts: 64 us -> 11 us
    all_to_all x18 -> x0, waiting for transfers between devices: 311 us -> none  [the longest x1 23.8 us: forward_three(): lax.all_to_all(second_tw[1], 'ctx', split_axis=0, concat_axis=1, tiled=True)]
    psum x1 -> x0, blocking collectives: 182 us -> none  [on_device(): grad_skip = lax.psum(skip_term, 'ctx')]
    all_to_all x18 -> x0, starting transfers between devices: 171 us -> none  [the longest x1 14.8 us: forward_three(): lax.all_to_all(as_blocks(first_sig, shards), 'ctx', split_axis=0, concat_...]
    pallas_call x0 -> x1, Pallas kernels: none -> 84.1 us  [on_device(): pl.pallas_call(kernel, out_shape=[jax.ShapeDtypeStruct(shape, bf16), jax....]
    dot_general x36 -> x0, matrix products: 59.6 us -> none  [the longest x3 9.79 us: block_section(): jnp.dot(cos_blocks, flattened, precision=exact_mode)]
    all_to_all x18 -> x0, local copies, waits for them, and re-layouts: 28.5 us -> none  [the longest x2 5.38 us: forward_three(): lax.all_to_all(first_tw[0], 'ctx', split_axis=0, concat_axis=1, tiled=True)]
    sub x6 -> x0, local copies, waits for them, and re-layouts: 11.4 us -> none  [the longest x3 5.96 us: inverse_blocks(): pieces.append(back_real * cos_twist - back_imag * sin_twist)]
    add x6 -> x0, local copies, waits for them, and re-layouts: 10.3 us -> none  [the longest x3 5.36 us: block_section(): real_part * cos_twist + imag_part * sin_twist]
  transfers between devices with their start and end apart: 18 -> 0, of which waited for: 17 -> 0; matrix products, arithmetic and copies ran while one was open for 11% -> 0% of each run, Pallas kernels for 0% -> 0%
where the time goes in v1:
time: 96.1 us; the launch traced here: 95.7 us
  Pallas kernels  84.1 us (88%)
  local copies, waits for them, and re-layouts  11 us (11%)
    pallas_call x1, Pallas kernels, on_device(): pl.pallas_call(kernel, out_shape=[jax.ShapeDtypeStruct(shape, bf16), jax....  84.1 us
    unnamed x21, local copies, waits for them, and re-layouts  11 us

profile of v1, /device:TPU:6, one launch (start us, length us, event | category | flops | bytes accessed | tf_op | source)
XLA Modules:
  0.0 95.7 jit_solution(12547368609758666818)
XLA Ops:
  0.6 0.0 copy-start
  0.6 1.0 %copy-done = f32[128,1024]{1,0:T(8,128)S(1)} copy-done((f32[128,1024]{1,0:T(8,128)S(1)}, f32[128,1024]{1,0:T(8,128)}, u32[]{:S(2)}) %copy-start) | copy-done | bytes 524312
  1.7 0.0 copy-start.1
  1.7 0.9 copy-done.1
  2.6 0.0 copy-start.2
  2.6 0.9 copy-done.2
  3.6 0.0 copy-start.3
  3.6 0.9 copy-done.3
  4.5 0.0 copy-start.4
  4.5 0.9 copy-done.4
  5.5 0.0 copy-start.5
  5.5 0.7 copy-done.5
  6.2 0.0 copy-start.6
  6.2 1.1 %copy-done.6 = bf16[1296,256]{1,0:T(8,128)(2,1)S(1)} copy-done((bf16[1296,256]{1,0:T(8,128)(2,1)S(1)}, bf16[1296,256]{1,0:T(8,128)(2,1)}, u32[]{:S(2)}) %copy-start.6) | copy-done | bytes 663576
  7.3 0.0 copy-start.7
  7.3 0.9 copy-done.7
  8.1 84.1 %hyena_backward.1 = (bf16[128,1024]{1,0:T(8,128)(2,1)S(1)}, bf16[128,1024]{1,0:T(8,128)(2,1)S(1)}, bf16[128,1024]{1,0:T(8,128)(2,1)S(1)}, f32[128,1024]{1,0:T(8,128)S(1)}, f32[8,128]{1,0:T(8,128)S(1)}) custom-call(bf16[128,1024]{1,0:T(8,128)(2,1)S(1)} %copy-done.1, bf16[128,1024]{1,0:T(8,128)(2,1)S(1)} %copy-done.2, bf16[128,1024]{1,0:T(8,128)(2,1)S(1)} %copy-done.3, ...), custom_call_target="tpu_custom_call" | custom-call | flops 4000000000 | bytes 3000000 | tf_op jit(solution)/shard_map/hyena_backward/pallas_call | solution.py:310
  92.2 0.7 copy.18
  92.9 0.7 copy.19
  93.6 0.7 copy.20
  94.3 0.8 copy.21
  95.1 0.6 copy.22
Async XLA Ops:
  0.6 1.0 %copy-start = (f32[128,1024]{1,0:T(8,128)S(1)}, f32[128,1024]{1,0:T(8,128)}, u32[]{:S(2)}) copy-start(f32[128,1024]{1,0:T(8,128)} %taps_hbm.1) | copy-start | bytes 1572868
  1.7 0.9 copy-start.1
  2.6 0.9 copy-start.2
  3.6 0.9 copy-start.3
  4.5 0.9 copy-start.4
  5.5 0.7 copy-start.5
  6.2 1.1 %copy-start.6 = (bf16[1296,256]{1,0:T(8,128)(2,1)S(1)}, bf16[1296,256]{1,0:T(8,128)(2,1)}, u32[]{:S(2)}) copy-start(bf16[1296,256]{1,0:T(8,128)(2,1)} %constant.4.clone.mats_hbm) | copy-start | bytes 1990660
  7.3 0.9 copy-start.7

commit v2 on v1

--- a/solution.py
+++ b/solution.py
@@ -3,7 +3,6 @@
 
 import jax
 import jax.numpy as jnp
-import ml_dtypes
 import numpy as np
 from jax import lax
 from jax.experimental import pallas as pl
@@ -22,12 +21,6 @@
 Z_ORDER = (1, 7, 3, 5, 2, 6, 4, 0)
 
 
-def split_bf16(values):
-    high = values.astype(ml_dtypes.bfloat16)
-    low = (values - high.astype(np.float64)).astype(ml_dtypes.bfloat16)
-    return high, low
-
-
 @functools.cache
 def tables():
     k1 = np.arange(HALF)[:, None]
@@ -35,32 +28,26 @@
     block = np.arange(BLOCKS)[None, :]
     angle = 2 * np.pi * ((k1 * block) % (2 * BLOCKS)) / (2 * BLOCKS)
     fwd_block = np.concatenate([np.cos(angle) * valid, -np.sin(angle) * valid])
-    high, low = split_bf16(fwd_block)
-    fwd_block = np.concatenate([high, high, low, low], axis=1)
+    fwd_block = np.concatenate([fwd_block] * 4, axis=1)
     weight = np.where((k1 == 0) | (k1 == BLOCKS), 1.0, 2.0) * valid / PERIOD
     inv_block = np.concatenate([np.cos(angle) * weight, -np.sin(angle) * weight]).T
-    inv_high, inv_low = split_bf16(inv_block)
-    pad = np.zeros((BLOCKS, 256 - 2 * HALF), ml_dtypes.bfloat16)
-    inv_block = np.concatenate(
-        [np.concatenate([inv_high, pad], 1), np.concatenate([inv_low, pad], 1)]
-    )
+    inv_block = np.pad(inv_block, ((0, 0), (0, 256 - 2 * HALF)))
     ids = np.arange(LANES)
     local = 2 * np.pi * ((ids[:, None] * ids[None, :]) % LANES) / LANES
     cos, sin = np.cos(local), np.sin(local)
     fwd_local = np.block([[cos, -sin], [sin, cos]])
     inv_local = np.block([[cos, sin], [-sin, cos]])
-    matrices = np.concatenate([fwd_block, *split_bf16(fwd_local), *split_bf16(inv_local), inv_block])
+    matrices = np.concatenate([fwd_block, fwd_local, inv_local, inv_block]).astype(np.float32)
     twist = 2 * np.pi * ((k1 * ids[None, :]) % PERIOD) / PERIOD
     twists = np.concatenate([np.cos(twist), np.sin(twist)]).astype(np.float32)
     return matrices, twists
 
 
-FWD_BLOCK = 0
-FWD_HIGH = 2 * HALF
-FWD_LOW = FWD_HIGH + 256
-INV_HIGH = FWD_LOW + 256
-INV_LOW = INV_HIGH + 256
-INV_BLOCK = INV_LOW + 256
+FWD_BLOCK = slice(0, 2 * HALF)
+FWD_LOCAL = slice(2 * HALF, 2 * HALF + 256)
+INV_LOCAL = slice(2 * HALF + 256, 2 * HALF + 512)
+INV_BLOCK = slice(2 * HALF + 512, 2 * HALF + 512 + BLOCKS)
+MATRIX_ROWS = INV_BLOCK.stop
 
 
 def halves(values):
@@ -75,7 +62,7 @@
 def kernel(
     query_hbm, key_hbm, value_hbm, grads_hbm, taps_hbm, skip_hbm, mats_hbm, twists_hbm,
     gq_hbm, gk_hbm, gv_hbm, gf_hbm, gs_hbm,
-    query, key, value, grads, taps, skip, mats, twists,
+    query, key, value, grads, taps, skip, mats, mats_high, mats_low, twists,
     gq, gk, gv, gf, gs,
     leaving, landed, spectra, rows_out, rows_in,
     load_sems, store_sems, send_sems, recv_sems,
@@ -164,6 +151,11 @@
 
     for load in loads[5:]:
         load.wait()
+    mats_high[...], mats_low[...] = halves(mats[...])
+    half_lanes = 2 * BLOCKS
+    fwd_block = jnp.concatenate(
+        [mats_high[FWD_BLOCK, :half_lanes], mats_low[FWD_BLOCK, half_lanes:]], axis=1
+    )
 
     def forward(s):
         signal = landed.at[s]
@@ -177,7 +169,7 @@
                 )
                 high, low = halves(both)
                 stacked = jnp.concatenate([high, low, high, low], axis=0)
-                parts = dot(mats[FWD_BLOCK : FWD_BLOCK + 2 * HALF, :], stacked)
+                parts = dot(fwd_block, stacked)
                 for i in range(2):
                     real, imag = parts[:HALF, columns(i)], parts[HALF:, columns(i)]
                     lines.append(
@@ -188,9 +180,9 @@
                     )
             high, low = halves(jnp.concatenate(lines, axis=0))
             spectra[s, group * ROWS : (group + 1) * ROWS, :] = (
-                dot(high, mats[FWD_HIGH : FWD_HIGH + 256, :])
-                + dot(low, mats[FWD_HIGH : FWD_HIGH + 256, :])
-                + dot(high, mats[FWD_LOW : FWD_LOW + 256, :])
+                dot(high, mats_high[FWD_LOCAL, :])
+                + dot(low, mats_high[FWD_LOCAL, :])
+                + dot(high, mats_low[FWD_LOCAL, :])
             )
 
     def inverse(s, left, right, conjugate):
@@ -206,9 +198,9 @@
                 product = [a_re * b_re - a_im * b_im, a_re * b_im + a_im * b_re]
             high, low = halves(jnp.concatenate(product, axis=1))
             back = (
-                dot(high, mats[INV_HIGH : INV_HIGH + 256, :])
-                + dot(low, mats[INV_HIGH : INV_HIGH + 256, :])
-                + dot(high, mats[INV_LOW : INV_LOW + 256, :])
+                dot(high, mats_high[INV_LOCAL, :])
+                + dot(low, mats_high[INV_LOCAL, :])
+                + dot(high, mats_low[INV_LOCAL, :])
             )
             for pair in range(GROUP // 2):
                 pieces = []
@@ -222,8 +214,8 @@
                         )
                     )
                 high, low = halves(jnp.concatenate(pieces, axis=1))
-                inv_high = mats[INV_BLOCK : INV_BLOCK + BLOCKS, 0 : 2 * HALF]
-                inv_low = mats[INV_BLOCK + BLOCKS : INV_BLOCK + 2 * BLOCKS, 0 : 2 * HALF]
+                inv_high = mats_high[INV_BLOCK, 0 : 2 * HALF]
+                inv_low = mats_low[INV_BLOCK, 0 : 2 * HALF]
                 values = dot(inv_high, high) + dot(inv_high, low) + dot(inv_low, high)
                 first = group * GROUP + 2 * pair
                 for i in range(2):
@@ -302,27 +294,42 @@
         store.wait()
 
 
+def hand_over(*refs):
+    given, taken, held, in_sems, out_sems = refs[:5], refs[5:10], refs[10:15], refs[15], refs[16]
+    reads = [pltpu.make_async_copy(given[i], held[i], in_sems.at[i]) for i in range(5)]
+    writes = [pltpu.make_async_copy(held[i], taken[i], out_sems.at[i]) for i in range(5)]
+    for read in reads:
+        read.start()
+    for read, write in zip(reads, writes, strict=True):
+        read.wait()
+        write.start()
+    for write in writes:
+        write.wait()
+
+
 def on_device(query_gate, key_gate, value_gate, out_grad, filter_taps, skip):
     matrices, twists = tables()
     shape = query_gate.shape
     assert shape == (LANES, WIDTH) and lax.axis_size("ctx") == BLOCKS
     bf16, f32 = jnp.bfloat16, jnp.float32
+    out_shape = [
+        jax.ShapeDtypeStruct(shape, bf16),
+        jax.ShapeDtypeStruct(shape, bf16),
+        jax.ShapeDtypeStruct(shape, bf16),
+        jax.ShapeDtypeStruct(shape, f32),
+        jax.ShapeDtypeStruct((8, LANES), f32),
+    ]
     outs = pl.pallas_call(
         kernel,
-        out_shape=[
-            jax.ShapeDtypeStruct(shape, bf16),
-            jax.ShapeDtypeStruct(shape, bf16),
-            jax.ShapeDtypeStruct(shape, bf16),
-            jax.ShapeDtypeStruct(shape, f32),
-            jax.ShapeDtypeStruct((8, LANES), f32),
-        ],
+        out_shape=out_shape,
         in_specs=[pl.BlockSpec(memory_space=pl.ANY)] * 8,
         out_specs=[pl.BlockSpec(memory_space=pl.ANY)] * 5,
         scratch_shapes=[
             *[pltpu.VMEM(shape, bf16)] * 4,
             pltpu.VMEM(shape, f32),
             pltpu.VMEM((1, WIDTH), f32),
-            pltpu.VMEM(matrices.shape, bf16),
+            pltpu.VMEM(matrices.shape, f32),
+            *[pltpu.VMEM(matrices.shape, bf16)] * 2,
             pltpu.VMEM(twists.shape, f32),
             *[pltpu.VMEM(shape, bf16)] * 3,
             pltpu.VMEM(shape, f32),
@@ -338,7 +345,7 @@
             pltpu.SemaphoreType.DMA((7,)),
         ],
         compiler_params=pltpu.CompilerParams(
-            collective_id=0, has_side_effects=True, vmem_limit_bytes=48 << 20
+            collective_id=0, has_side_effects=True, vmem_limit_bytes=63 << 20
         ),
         cost_estimate=pl.CostEstimate(
             flops=4 * 10**9, bytes_accessed=3 * 10**6, transcendentals=0
@@ -348,6 +355,20 @@
         query_gate, key_gate, value_gate, out_grad, filter_taps, skip.reshape(1, WIDTH),
         jnp.asarray(matrices), jnp.asarray(twists),
     )
+    outs = pl.pallas_call(
+        hand_over,
+        out_shape=out_shape,
+        in_specs=[pl.BlockSpec(memory_space=pl.ANY)] * 5,
+        out_specs=[pl.BlockSpec(memory_space=pl.ANY)] * 5,
+        scratch_shapes=[
+            *[pltpu.VMEM(out.shape, out.dtype) for out in out_shape],
+            pltpu.SemaphoreType.DMA((5,)),
+            pltpu.SemaphoreType.DMA((5,)),
+        ],
+        compiler_params=pltpu.CompilerParams(vmem_limit_bytes=63 << 20),
+        cost_estimate=pl.CostEstimate(flops=0, bytes_accessed=3 * 10**6, transcendentals=0),
+        name="hand_over",
+    )(*outs)
     return (*outs[:4], outs[4].reshape(WIDTH))
 
 

time: 96.1 us -> 87.3 us (0.908)
  local copies, waits for them, and re-layouts: 11 us -> 0 us
  Pallas kernels: 84.1 us -> 86.6 us
    unnamed x21 -> x0, local copies, waits for them, and re-layouts: 11 us -> none
    pallas_call x1 -> x2, Pallas kernels: 84.1 us -> 86.6 us  [the longest x1 84.4 us: on_device(): pl.pallas_call(kernel, out_shape=out_shape, in_specs=[pl.BlockSpec(memory...]
where the time goes in v2:
time: 87.3 us; the launch traced here: 87.2 us
  Pallas kernels  86.6 us (99%)
    pallas_call x1, Pallas kernels, on_device(): pl.pallas_call(kernel, out_shape=out_shape, in_specs=[pl.BlockSpec(memory...  84.4 us
    pallas_call x1, Pallas kernels, on_device(): pl.pallas_call(hand_over, out_shape=out_shape, in_specs=[pl.BlockSpec(mem...  2.16 us

profile of v2, /device:TPU:6, one launch (start us, length us, event | category | flops | bytes accessed | tf_op | source)
XLA Modules:
  0.0 87.2 jit_solution(2844617933680571626)
XLA Ops:
  0.6 84.4 %hyena_backward.1 = (bf16[128,1024]{1,0:T(8,128)(2,1)}, bf16[128,1024]{1,0:T(8,128)(2,1)}, bf16[128,1024]{1,0:T(8,128)(2,1)}, f32[128,1024]{1,0:T(8,128)}, f32[8,128]{1,0:T(8,128)}) custom-call(bf16[128,1024]{1,0:T(8,128)(2,1)} %query_hbm.1, bf16[128,1024]{1,0:T(8,128)(2,1)} %key_hbm.1, bf16[128,1024]{1,0:T(8,128)(2,1)} %value_hbm.1, ...), custom_call_target="tpu_custom_call" | custom-call | flops 4000000000 | bytes 3000000 | tf_op jit(solution)/shard_map/hyena_backward/pallas_call | solution.py:322
  85.0 2.2 %hand_over.1 = (bf16[128,1024]{1,0:T(8,128)(2,1)}, bf16[128,1024]{1,0:T(8,128)(2,1)}, bf16[128,1024]{1,0:T(8,128)(2,1)}, f32[128,1024]{1,0:T(8,128)}, f32[8,128]{1,0:T(8,128)}) custom-call(bf16[128,1024]{1,0:T(8,128)(2,1)} %get-tuple-element.15.refs_0_, bf16[128,1024]{1,0:T(8,128)(2,1)} %get-tuple-element.16.refs_1_, ...), custom_call_target="tpu_custom_call" | custom-call | bytes 3000000 | tf_op jit(solution)/shard_map/hand_over/pallas_call | solution.py:358

commit v3 on v2

--- a/solution.py
+++ b/solution.py
@@ -61,11 +61,10 @@
 
 def kernel(
     query_hbm, key_hbm, value_hbm, grads_hbm, taps_hbm, skip_hbm, mats_hbm, twists_hbm,
-    gq_hbm, gk_hbm, gv_hbm, gf_hbm, gs_hbm,
+    gq, gk, gv, gf, gs,
     query, key, value, grads, taps, skip, mats, mats_high, mats_low, twists,
-    gq, gk, gv, gf, gs,
     leaving, landed, spectra, rows_out, rows_in,
-    load_sems, store_sems, send_sems, recv_sems,
+    load_sems, send_sems, recv_sems, row_send_sems, row_recv_sems,
 ):
     me = lax.axis_index("ctx")
     dp = lax.axis_index("dp")
@@ -78,17 +77,19 @@
              (query_hbm, query), (twists_hbm, twists), (mats_hbm, mats), (skip_hbm, skip))
         )
     ]
-    for load in loads:
+    loads[0].start()
+
+    barrier = pltpu.get_barrier_semaphore()
+    planes = [((my_z + dz) % 8) * 4 for dz in range(8)]
+    spots = [((my_x + xy // 4) % 2) * 32 + (my_y + xy) % 4 for xy in range(8)]
+    for dz in (4, 3, 5, 2, 6, 1, 7, 0):
+        for xy in (6, 5, 7, 4, 2, 1, 3, 0):
+            if dz or xy:
+                pl.semaphore_signal(
+                    barrier, inc=1, device_id=(dp, planes[dz] + spots[xy]), device_id_type=MESH
+                )
+    for load in loads[1:]:
         load.start()
-
-    barrier = pltpu.get_barrier_semaphore()
-
-    def greet(i, carry):
-        there = lax.rem(me + 1 + i, BLOCKS)
-        pl.semaphore_signal(barrier, inc=1, device_id=(dp, there), device_id_type=MESH)
-        return carry
-
-    lax.fori_loop(0, BLOCKS - 1, greet, 0)
 
     def rows_of(device):
         return pl.ds(pl.multiple_of(device * OWN, OWN), OWN)
@@ -135,15 +136,44 @@
     pl.semaphore_wait(barrier, BLOCKS - 1)
     send_signal(0)
 
-    loads[1].wait()
-    loads[2].wait()
+    my_row, my_group = me % 8, me // 8
+    root_scale = 1.0 / math.sqrt(BLOCKS * LANES)
+
+    def send_rows(step, source_of, device_of, slot):
+        for i in range(1, 8):
+            pltpu.make_async_remote_copy(
+                src_ref=source_of(i),
+                dst_ref=rows_in.at[step, slot],
+                send_sem=row_send_sems.at[step],
+                recv_sem=row_recv_sems.at[step],
+                device_id=(dp, device_of(i)),
+                device_id_type=MESH,
+            ).start()
+
+    def wait_rows(step, sems):
+        most = pl.ds(0, 7)
+        pltpu.make_async_copy(rows_in.at[step, most], rows_in.at[step, most], sems.at[step]).wait()
+
+    def in_group(i):
+        return my_group * 8 + (my_row + i) % 8
+
+    def across(i):
+        return ((my_group + i) % 8) * 8 + my_row
+
+    for load in loads[1:5]:
+        load.wait()
+    for j in range(WIDTH // LANES):
+        gated = key[:, columns(j)].astype(jnp.float32) * value[:, columns(j)].astype(jnp.float32)
+        conv_grad = grads[:, columns(j)].astype(jnp.float32) * query[:, columns(j)].astype(jnp.float32)
+        rows_out[j] = jnp.sum(gated * conv_grad, axis=0, keepdims=True)
+    send_rows(0, lambda i: rows_out.at[(my_row + i) % 8], in_group, my_row)
+    rows_in[0, pl.ds(my_row, 1)] = rows_out[pl.ds(my_row, 1)]
+
     for j in range(WIDTH // LANES):
         gated = key[:, columns(j)].astype(jnp.float32) * value[:, columns(j)].astype(jnp.float32)
         leaving[1, columns(j), :] = gated.T
     send_signal(1)
 
-    loads[3].wait()
-    loads[4].wait()
     for j in range(WIDTH // LANES):
         conv_grad = grads[:, columns(j)].astype(jnp.float32) * query[:, columns(j)].astype(jnp.float32)
         leaving[2, columns(j), :] = conv_grad.T
@@ -223,47 +253,35 @@
 
     wait_bytes(0, recv_sems)
     forward(0)
+    wait_rows(0, row_recv_sems)
+    rows_out[8] = jnp.sum(rows_in[0], axis=0)
+    send_rows(1, lambda i: rows_out.at[8], across, my_group)
+    rows_in[1, pl.ds(my_group, 1)] = rows_out[pl.ds(8, 1)]
+
     wait_bytes(1, recv_sems)
     forward(1)
     inverse(0, 0, 1, False)
     send_signal(3)
+
     wait_bytes(2, recv_sems)
+    wait_rows(1, row_recv_sems)
+    rows_out[9] = jnp.sum(rows_in[1], axis=0) * root_scale
+    send_rows(2, lambda i: rows_out.at[9], in_group, my_row)
+    rows_in[2, pl.ds(my_row, 1)] = rows_out[pl.ds(9, 1)]
     forward(2)
     inverse(1, 0, 2, True)
     send_signal(4)
     inverse(2, 1, 2, True)
     send_signal(5)
 
-    total = jnp.zeros((OWN, LANES), jnp.float32)
-    for b in range(BLOCKS):
-        total = total + landed[1, b * OWN : (b + 1) * OWN, :] * landed[2, b * OWN : (b + 1) * OWN, :]
-    total = jnp.sum(total, axis=1, keepdims=True)
-    lane = lax.broadcasted_iota(jnp.int32, (OWN, LANES), 1)
-    channel = lax.broadcasted_iota(jnp.int32, (OWN, LANES), 0)
-    placed = jnp.where(lane == channel + (me % 8) * OWN, total, 0.0)
-    root_scale = 1.0 / math.sqrt(BLOCKS * LANES)
-    rows_out[...] = jnp.sum(placed, axis=0, keepdims=True) * root_scale
-    rows_in[pl.ds(me, 1)] = rows_out[...].reshape(1, 1, LANES)
-
-    def send_row(there):
-        pltpu.make_async_remote_copy(
-            src_ref=rows_out,
-            dst_ref=rows_in.at[me],
-            send_sem=send_sems.at[6],
-            recv_sem=recv_sems.at[6],
-            device_id=(dp, there),
-            device_id_type=MESH,
-        ).start()
-
-    to_all(send_row)
-
     wait_bytes(3, recv_sems)
     for j in range(WIDTH // LANES):
         gated = key[:, columns(j)].astype(jnp.float32) * value[:, columns(j)].astype(jnp.float32)
         conv = landed[3, columns(j), :].T + skip[:, columns(j)] * gated
         gq[:, columns(j)] = (grads[:, columns(j)].astype(jnp.float32) * conv).astype(jnp.bfloat16)
-    stores = [pltpu.make_async_copy(gq, gq_hbm, store_sems.at[0])]
-    stores[0].start()
+    wait_rows(2, row_recv_sems)
+    for j in range(8):
+        gs[j : j + 1, :] = rows_in[2, j]
 
     wait_bytes(4, recv_sems)
     for j in range(WIDTH // LANES):
@@ -271,37 +289,21 @@
         back = landed[4, columns(j), :].T + skip[:, columns(j)] * conv_grad
         gk[:, columns(j)] = (back * value[:, columns(j)].astype(jnp.float32)).astype(jnp.bfloat16)
         gv[:, columns(j)] = (back * key[:, columns(j)].astype(jnp.float32)).astype(jnp.bfloat16)
-    for i, (src, dst) in enumerate(((gk, gk_hbm), (gv, gv_hbm))):
-        stores.append(pltpu.make_async_copy(src, dst, store_sems.at[1 + i]))
-        stores[-1].start()
 
     wait_bytes(5, recv_sems)
     for j in range(WIDTH // LANES):
         gf[:, columns(j)] = landed[5, columns(j), :].T * root_scale
-    stores.append(pltpu.make_async_copy(gf, gf_hbm, store_sems.at[3]))
-    stores[-1].start()
-
-    most = pl.ds(0, BLOCKS - 1)
-    pltpu.make_async_copy(rows_in.at[most], rows_in.at[most], recv_sems.at[6]).wait()
-    gs[...] = jnp.sum(rows_in[...].reshape(8, 8, LANES), axis=1)
-    stores.append(pltpu.make_async_copy(gs, gs_hbm, store_sems.at[4]))
-    stores[-1].start()
 
     for s in range(6):
         wait_bytes(s, send_sems)
-    pltpu.make_async_copy(rows_in.at[most], rows_in.at[most], send_sems.at[6]).wait()
-    for store in stores:
-        store.wait()
+    for step in range(3):
+        wait_rows(step, row_send_sems)
 
 
 def hand_over(*refs):
-    given, taken, held, in_sems, out_sems = refs[:5], refs[5:10], refs[10:15], refs[15], refs[16]
-    reads = [pltpu.make_async_copy(given[i], held[i], in_sems.at[i]) for i in range(5)]
-    writes = [pltpu.make_async_copy(held[i], taken[i], out_sems.at[i]) for i in range(5)]
-    for read in reads:
-        read.start()
-    for read, write in zip(reads, writes, strict=True):
-        read.wait()
+    given, taken, sems = refs[:5], refs[5:10], refs[10]
+    writes = [pltpu.make_async_copy(given[i], taken[i], sems.at[i]) for i in range(5)]
+    for write in writes:
         write.start()
     for write in writes:
         write.wait()
@@ -321,9 +323,9 @@
     ]
     outs = pl.pallas_call(
         kernel,
-        out_shape=out_shape,
+        out_shape=[pltpu.VMEM(out.shape, out.dtype) for out in out_shape],
         in_specs=[pl.BlockSpec(memory_space=pl.ANY)] * 8,
-        out_specs=[pl.BlockSpec(memory_space=pl.ANY)] * 5,
+        out_specs=[pl.BlockSpec(memory_space=pltpu.VMEM)] * 5,
         scratch_shapes=[
             *[pltpu.VMEM(shape, bf16)] * 4,
             pltpu.VMEM(shape, f32),
@@ -331,44 +333,43 @@
             pltpu.VMEM(matrices.shape, f32),
             *[pltpu.VMEM(matrices.shape, bf16)] * 2,
             pltpu.VMEM(twists.shape, f32),
-            *[pltpu.VMEM(shape, bf16)] * 3,
-            pltpu.VMEM(shape, f32),
-            pltpu.VMEM((8, LANES), f32),
             pltpu.VMEM((6, WIDTH, LANES), f32),
             pltpu.VMEM((6, WIDTH, LANES), f32),
             pltpu.VMEM((3, OWN * HALF, 2 * LANES), f32),
-            pltpu.VMEM((1, LANES), f32),
-            pltpu.VMEM((BLOCKS, 1, LANES), f32),
+            pltpu.VMEM((10, 1, LANES), f32),
+            pltpu.VMEM((3, 8, 1, LANES), f32),
             pltpu.SemaphoreType.DMA((8,)),
-            pltpu.SemaphoreType.DMA((5,)),
-            pltpu.SemaphoreType.DMA((7,)),
-            pltpu.SemaphoreType.DMA((7,)),
+            pltpu.SemaphoreType.DMA((6,)),
+            pltpu.SemaphoreType.DMA((6,)),
+            pltpu.SemaphoreType.DMA((3,)),
+            pltpu.SemaphoreType.DMA((3,)),
         ],
         compiler_params=pltpu.CompilerParams(
-            collective_id=0, has_side_effects=True, vmem_limit_bytes=63 << 20
+            collective_id=0, has_side_effects=True, vmem_limit_bytes=40 << 20
         ),
         cost_estimate=pl.CostEstimate(
             flops=4 * 10**9, bytes_accessed=3 * 10**6, transcendentals=0
         ),
         name="hyena_backward",
     )(
-        query_gate, key_gate, value_gate, out_grad, filter_taps, skip.reshape(1, WIDTH),
-        jnp.asarray(matrices), jnp.asarray(twists),
+        *[
+            pltpu.with_memory_space_constraint(operand, pltpu.HBM)
+            for operand in (
+                query_gate, key_gate, value_gate, out_grad, filter_taps, skip.reshape(1, WIDTH),
+                jnp.asarray(matrices), jnp.asarray(twists),
+            )
+        ]
     )
     outs = pl.pallas_call(
         hand_over,
-        out_shape=out_shape,
+        out_shape=[pltpu.HBM(out.shape, out.dtype) for out in out_shape],
         in_specs=[pl.BlockSpec(memory_space=pl.ANY)] * 5,
         out_specs=[pl.BlockSpec(memory_space=pl.ANY)] * 5,
-        scratch_shapes=[
-            *[pltpu.VMEM(out.shape, out.dtype) for out in out_shape],
-            pltpu.SemaphoreType.DMA((5,)),
-            pltpu.SemaphoreType.DMA((5,)),
-        ],
-        compiler_params=pltpu.CompilerParams(vmem_limit_bytes=63 << 20),
+        scratch_shapes=[pltpu.SemaphoreType.DMA((5,))],
+        compiler_params=pltpu.CompilerParams(vmem_limit_bytes=8 << 20),
         cost_estimate=pl.CostEstimate(flops=0, bytes_accessed=3 * 10**6, transcendentals=0),
         name="hand_over",
-    )(*outs)
+    )(*[pltpu.with_memory_space_constraint(out, pltpu.VMEM) for out in outs])
     return (*outs[:4], outs[4].reshape(WIDTH))
 
 

time: 87.3 us -> 84.4 us (0.967)
  Pallas kernels: 86.6 us -> 82.8 us
    pallas_call x2, Pallas kernels: 86.6 us -> 82.8 us  [the longest x1 81.7 us: on_device(): pl.pallas_call(kernel, out_shape=[pltpu.VMEM(out.shape, out.dtype) for ou...]
where the time goes in v3:
time: 84.4 us; the launch traced here: 83.5 us
  Pallas kernels  82.8 us (98%)
    pallas_call x1, Pallas kernels, on_device(): pl.pallas_call(kernel, out_shape=[pltpu.VMEM(out.shape, out.dtype) for ou...  81.7 us

profile of v3, /device:TPU:6, one launch (start us, length us, event | category | flops | bytes accessed | tf_op | source)
XLA Modules:
  0.0 83.5 jit_solution(9237706694908645165)
XLA Ops:
  0.6 81.7 %hyena_backward.1 = (bf16[128,1024]{1,0:T(8,128)(2,1)S(1)}, bf16[128,1024]{1,0:T(8,128)(2,1)S(1)}, bf16[128,1024]{1,0:T(8,128)(2,1)S(1)}, f32[128,1024]{1,0:T(8,128)S(1)}, f32[8,128]{1,0:T(8,128)S(1)}) custom-call(bf16[128,1024]{1,0:T(8,128)(2,1)} %query_hbm.1, bf16[128,1024]{1,0:T(8,128)(2,1)} %key_hbm.1, bf16[128,1024]{1,0:T(8,128)(2,1)} %value_hbm.1, ...), custom_call_target="tpu_custom_call" | custom-call | flops 4000000000 | bytes 3000000 | tf_op jit(solution)/shard_map/hyena_backward/pallas_call | solution.py:324
  82.4 1.1 %hand_over.1 = (bf16[128,1024]{1,0:T(8,128)(2,1)}, bf16[128,1024]{1,0:T(8,128)(2,1)}, bf16[128,1024]{1,0:T(8,128)(2,1)}, f32[128,1024]{1,0:T(8,128)}, f32[8,128]{1,0:T(8,128)}) custom-call(bf16[128,1024]{1,0:T(8,128)(2,1)S(1)} %get-tuple-element.15.refs_0_, bf16[128,1024]{1,0:T(8,128)(2,1)S(1)} %get-tuple-element.16.refs_1_, ...), custom_call_target="tpu_custom_call" | custom-call | bytes 3000000 | tf_op jit(solution)/shard_map/hand_over/pallas_call | solution.py:363

commit v4 on v3

--- a/solution.py
+++ b/solution.py
@@ -28,7 +28,7 @@
     block = np.arange(BLOCKS)[None, :]
     angle = 2 * np.pi * ((k1 * block) % (2 * BLOCKS)) / (2 * BLOCKS)
     fwd_block = np.concatenate([np.cos(angle) * valid, -np.sin(angle) * valid])
-    fwd_block = np.concatenate([fwd_block] * 4, axis=1)
+    fwd_block = np.pad(fwd_block, ((0, 0), (0, 256 - BLOCKS)))
     weight = np.where((k1 == 0) | (k1 == BLOCKS), 1.0, 2.0) * valid / PERIOD
     inv_block = np.concatenate([np.cos(angle) * weight, -np.sin(angle) * weight]).T
     inv_block = np.pad(inv_block, ((0, 0), (0, 256 - 2 * HALF)))
@@ -47,22 +47,18 @@
 FWD_LOCAL = slice(2 * HALF, 2 * HALF + 256)
 INV_LOCAL = slice(2 * HALF + 256, 2 * HALF + 512)
 INV_BLOCK = slice(2 * HALF + 512, 2 * HALF + 512 + BLOCKS)
-MATRIX_ROWS = INV_BLOCK.stop
-
-
-def halves(values):
-    high = values.astype(jnp.bfloat16)
-    return high, (values - high.astype(jnp.float32)).astype(jnp.bfloat16)
 
 
 def dot(left, right):
-    return jnp.dot(left, right, preferred_element_type=jnp.float32)
+    return jnp.dot(
+        left, right, precision=lax.Precision.HIGHEST, preferred_element_type=jnp.float32
+    )
 
 
 def kernel(
     query_hbm, key_hbm, value_hbm, grads_hbm, taps_hbm, skip_hbm, mats_hbm, twists_hbm,
     gq, gk, gv, gf, gs,
-    query, key, value, grads, taps, skip, mats, mats_high, mats_low, twists,
+    query, key, value, grads, taps, skip, mats, twists,
     leaving, landed, spectra, rows_out, rows_in,
     load_sems, send_sems, recv_sems, row_send_sems, row_recv_sems,
 ):
@@ -181,11 +177,6 @@
 
     for load in loads[5:]:
         load.wait()
-    mats_high[...], mats_low[...] = halves(mats[...])
-    half_lanes = 2 * BLOCKS
-    fwd_block = jnp.concatenate(
-        [mats_high[FWD_BLOCK, :half_lanes], mats_low[FWD_BLOCK, half_lanes:]], axis=1
-    )
 
     def forward(s):
         signal = landed.at[s]
@@ -197,9 +188,7 @@
                 both = jnp.concatenate(
                     [signal[pl.ds(first + i, BLOCKS, stride=OWN), :] for i in range(2)], axis=1
                 )
-                high, low = halves(both)
-                stacked = jnp.concatenate([high, low, high, low], axis=0)
-                parts = dot(fwd_block, stacked)
+                parts = dot(mats[FWD_BLOCK, 0:BLOCKS], both)
                 for i in range(2):
                     real, imag = parts[:HALF, columns(i)], parts[HALF:, columns(i)]
                     lines.append(
@@ -208,11 +197,8 @@
                             axis=1,
                         )
                     )
-            high, low = halves(jnp.concatenate(lines, axis=0))
-            spectra[s, group * ROWS : (group + 1) * ROWS, :] = (
-                dot(high, mats_high[FWD_LOCAL, :])
-                + dot(low, mats_high[FWD_LOCAL, :])
-                + dot(high, mats_low[FWD_LOCAL, :])
+            spectra[s, group * ROWS : (group + 1) * ROWS, :] = dot(
+                jnp.concatenate(lines, axis=0), mats[FWD_LOCAL, :]
             )
 
     def inverse(s, left, right, conjugate):
@@ -226,12 +212,7 @@
                 product = [a_re * b_re + a_im * b_im, a_re * b_im - a_im * b_re]
             else:
                 product = [a_re * b_re - a_im * b_im, a_re * b_im + a_im * b_re]
-            high, low = halves(jnp.concatenate(product, axis=1))
-            back = (
-                dot(high, mats_high[INV_LOCAL, :])
-                + dot(low, mats_high[INV_LOCAL, :])
-                + dot(high, mats_low[INV_LOCAL, :])
-            )
+            back = dot(jnp.concatenate(product, axis=1), mats[INV_LOCAL, :])
             for pair in range(GROUP // 2):
                 pieces = []
                 for i in range(2):
@@ -243,10 +224,7 @@
                             axis=0,
                         )
                     )
-                high, low = halves(jnp.concatenate(pieces, axis=1))
-                inv_high = mats_high[INV_BLOCK, 0 : 2 * HALF]
-                inv_low = mats_low[INV_BLOCK, 0 : 2 * HALF]
-                values = dot(inv_high, high) + dot(inv_high, low) + dot(inv_low, high)
+                values = dot(mats[INV_BLOCK, 0 : 2 * HALF], jnp.concatenate(pieces, axis=1))
                 first = group * GROUP + 2 * pair
                 for i in range(2):
                     result[pl.ds(first + i, BLOCKS, stride=OWN), :] = values[:, columns(i)]
@@ -331,7 +309,6 @@
             pltpu.VMEM(shape, f32),
             pltpu.VMEM((1, WIDTH), f32),
             pltpu.VMEM(matrices.shape, f32),
-            *[pltpu.VMEM(matrices.shape, bf16)] * 2,
             pltpu.VMEM(twists.shape, f32),
             pltpu.VMEM((6, WIDTH, LANES), f32),
             pltpu.VMEM((6, WIDTH, LANES), f32),

time: 84.4 us -> 84.7 us (level)
  no operation moved by 1% of the time
where the time goes in v4:
time: 84.7 us; the launch traced here: 83.6 us
  Pallas kernels  82.8 us (98%)
    pallas_call x1, Pallas kernels, on_device(): pl.pallas_call(kernel, out_shape=[pltpu.VMEM(out.shape, out.dtype) for ou...  81.7 us

profile of v4, /device:TPU:6, one launch (start us, length us, event | category | flops | bytes accessed | tf_op | source)
XLA Modules:
  0.0 83.6 jit_solution(11638215879557730730)
XLA Ops:
  0.6 81.7 %hyena_backward.1 = (bf16[128,1024]{1,0:T(8,128)(2,1)S(1)}, bf16[128,1024]{1,0:T(8,128)(2,1)S(1)}, bf16[128,1024]{1,0:T(8,128)(2,1)S(1)}, f32[128,1024]{1,0:T(8,128)S(1)}, f32[8,128]{1,0:T(8,128)S(1)}) custom-call(bf16[128,1024]{1,0:T(8,128)(2,1)} %query_hbm.1, bf16[128,1024]{1,0:T(8,128)(2,1)} %key_hbm.1, bf16[128,1024]{1,0:T(8,128)(2,1)} %value_hbm.1, ...), custom_call_target="tpu_custom_call" | custom-call | flops 4000000000 | bytes 3000000 | tf_op jit(solution)/shard_map/hyena_backward/pallas_call | solution.py:302
  82.4 1.1 %hand_over.1 = (bf16[128,1024]{1,0:T(8,128)(2,1)}, bf16[128,1024]{1,0:T(8,128)(2,1)}, bf16[128,1024]{1,0:T(8,128)(2,1)}, f32[128,1024]{1,0:T(8,128)}, f32[8,128]{1,0:T(8,128)}) custom-call(bf16[128,1024]{1,0:T(8,128)(2,1)S(1)} %get-tuple-element.15.refs_0_, bf16[128,1024]{1,0:T(8,128)(2,1)S(1)} %get-tuple-element.16.refs_1_, ...), custom_call_target="tpu_custom_call" | custom-call | bytes 3000000 | tf_op jit(solution)/shard_map/hand_over/pallas_call | solution.py:340

commit v5 on v4

--- a/solution.py
+++ b/solution.py
@@ -18,7 +18,7 @@
 HALF = 72
 GROUP = 4
 ROWS = GROUP * HALF
-Z_ORDER = (1, 7, 3, 5, 2, 6, 4, 0)
+Z_ORDER = (4, 3, 5, 2, 6, 1, 7)
 
 
 @functools.cache
@@ -60,7 +60,7 @@
     gq, gk, gv, gf, gs,
     query, key, value, grads, taps, skip, mats, twists,
     leaving, landed, spectra, rows_out, rows_in,
-    load_sems, send_sems, recv_sems, row_send_sems, row_recv_sems,
+    load_sems, send_sems, recv_sems, row_send_sems, row_recv_sems, planes_in,
 ):
     me = lax.axis_index("ctx")
     dp = lax.axis_index("dp")
@@ -78,46 +78,44 @@
     barrier = pltpu.get_barrier_semaphore()
     planes = [((my_z + dz) % 8) * 4 for dz in range(8)]
     spots = [((my_x + xy // 4) % 2) * 32 + (my_y + xy) % 4 for xy in range(8)]
-    for dz in (4, 3, 5, 2, 6, 1, 7, 0):
-        for xy in (6, 5, 7, 4, 2, 1, 3, 0):
-            if dz or xy:
-                pl.semaphore_signal(
-                    barrier, inc=1, device_id=(dp, planes[dz] + spots[xy]), device_id_type=MESH
-                )
+    column = [planes[dz] + spots[0] for dz in Z_ORDER]
+    plane = [planes[0] + spots[xy] for xy in (6, 5, 7, 4, 2, 1, 3)]
+    for there in column + plane:
+        pl.semaphore_signal(barrier, inc=1, device_id=(dp, there), device_id_type=MESH)
     for load in loads[1:]:
         load.start()
 
     def rows_of(device):
         return pl.ds(pl.multiple_of(device * OWN, OWN), OWN)
 
-    def to_all(send_one):
+    def send_one(s, there):
+        pltpu.make_async_remote_copy(
+            src_ref=leaving.at[s, rows_of(there), :],
+            dst_ref=landed.at[s, rows_of(me), :],
+            send_sem=send_sems.at[s],
+            recv_sem=recv_sems.at[s],
+            device_id=(dp, there),
+            device_id_type=MESH,
+        ).start()
+
+    def send_near(s):
+        for there in column + plane:
+            send_one(s, there)
+        landed[s, rows_of(me), :] = leaving[s, rows_of(me), :]
+
+    def send_far(s):
         def body(j, carry):
             for zi, dz in enumerate(Z_ORDER):
-                xy = (j + zi) % 8 if dz else j
-                there = ((my_x + xy // 4) % 2) * 32 + ((my_z + dz) % 8) * 4 + (my_y + xy) % 4
-                if dz:
-                    send_one(there)
-                else:
-                    @pl.when(j > 0)
-                    def _():
-                        send_one(there)
+                xy = (j + zi) % 7 + 1
+                spot = ((my_x + xy // 4) % 2) * 32 + (my_y + xy) % 4
+                send_one(s, planes[dz] + spot)
             return carry
 
-        lax.fori_loop(0, 8, body, 0)
+        lax.fori_loop(0, 7, body, 0)
 
     def send_signal(s):
-        def one(there):
-            pltpu.make_async_remote_copy(
-                src_ref=leaving.at[s, rows_of(there), :],
-                dst_ref=landed.at[s, rows_of(me), :],
-                send_sem=send_sems.at[s],
-                recv_sem=recv_sems.at[s],
-                device_id=(dp, there),
-                device_id_type=MESH,
-            ).start()
-
-        to_all(one)
-        landed[s, rows_of(me), :] = leaving[s, rows_of(me), :]
+        send_near(s)
+        send_far(s)
 
     def wait_bytes(s, sems):
         most = pl.ds(0, (BLOCKS - 1) * OWN)
@@ -129,8 +127,21 @@
     loads[0].wait()
     for j in range(WIDTH // LANES):
         leaving[0, columns(j), :] = taps[:, columns(j)].T
-    pl.semaphore_wait(barrier, BLOCKS - 1)
-    send_signal(0)
+    pl.semaphore_wait(barrier, len(column) + len(plane))
+    for there in column:
+        pl.semaphore_signal(planes_in, inc=1, device_id=(dp, there), device_id_type=MESH)
+    send_near(0)
+
+    for load in loads[1:5]:
+        load.wait()
+    for j in range(WIDTH // LANES):
+        gated = key[:, columns(j)].astype(jnp.float32) * value[:, columns(j)].astype(jnp.float32)
+        leaving[1, columns(j), :] = gated.T
+    send_near(1)
+    for j in range(WIDTH // LANES):
+        conv_grad = grads[:, columns(j)].astype(jnp.float32) * query[:, columns(j)].astype(jnp.float32)
+        leaving[2, columns(j), :] = conv_grad.T
+    send_near(2)
 
     my_row, my_group = me % 8, me // 8
     root_scale = 1.0 / math.sqrt(BLOCKS * LANES)
@@ -156,24 +167,17 @@
     def across(i):
         return ((my_group + i) % 8) * 8 + my_row
 
-    for load in loads[1:5]:
-        load.wait()
     for j in range(WIDTH // LANES):
         gated = key[:, columns(j)].astype(jnp.float32) * value[:, columns(j)].astype(jnp.float32)
         conv_grad = grads[:, columns(j)].astype(jnp.float32) * query[:, columns(j)].astype(jnp.float32)
         rows_out[j] = jnp.sum(gated * conv_grad, axis=0, keepdims=True)
+    rows_in[0, pl.ds(my_row, 1)] = rows_out[pl.ds(my_row, 1)]
+
+    pl.semaphore_wait(planes_in, len(column))
+    send_far(0)
     send_rows(0, lambda i: rows_out.at[(my_row + i) % 8], in_group, my_row)
-    rows_in[0, pl.ds(my_row, 1)] = rows_out[pl.ds(my_row, 1)]
-
-    for j in range(WIDTH // LANES):
-        gated = key[:, columns(j)].astype(jnp.float32) * value[:, columns(j)].astype(jnp.float32)
-        leaving[1, columns(j), :] = gated.T
-    send_signal(1)
-
-    for j in range(WIDTH // LANES):
-        conv_grad = grads[:, columns(j)].astype(jnp.float32) * query[:, columns(j)].astype(jnp.float32)
-        leaving[2, columns(j), :] = conv_grad.T
-    send_signal(2)
+    send_far(1)
+    send_far(2)
 
     for load in loads[5:]:
         load.wait()
@@ -320,6 +324,7 @@
             pltpu.SemaphoreType.DMA((6,)),
             pltpu.SemaphoreType.DMA((3,)),
             pltpu.SemaphoreType.DMA((3,)),
+            pltpu.SemaphoreType.REGULAR,
         ],
         compiler_params=pltpu.CompilerParams(
             collective_id=0, has_side_effects=True, vmem_limit_bytes=40 << 20

time: 84.7 us -> 83.2 us (0.982)
  no operation moved by 1% of the time
where the time goes in v5:
time: 83.2 us; the launch traced here: 82.9 us
  Pallas kernels  82.1 us (99%)
    pallas_call x1, Pallas kernels, on_device(): pl.pallas_call(kernel, out_shape=[pltpu.VMEM(out.shape, out.dtype) for ou...  81 us

profile of v5, /device:TPU:6, one launch (start us, length us, event | category | flops | bytes accessed | tf_op | source)
XLA Modules:
  0.0 82.9 jit_solution(10905226948319359020)
XLA Ops:
  0.6 81.0 %hyena_backward.1 = (bf16[128,1024]{1,0:T(8,128)(2,1)S(1)}, bf16[128,1024]{1,0:T(8,128)(2,1)S(1)}, bf16[128,1024]{1,0:T(8,128)(2,1)S(1)}, f32[128,1024]{1,0:T(8,128)S(1)}, f32[8,128]{1,0:T(8,128)S(1)}) custom-call(bf16[128,1024]{1,0:T(8,128)(2,1)} %query_hbm.1, bf16[128,1024]{1,0:T(8,128)(2,1)} %key_hbm.1, bf16[128,1024]{1,0:T(8,128)(2,1)} %value_hbm.1, ...), custom_call_target="tpu_custom_call" | custom-call | flops 4000000000 | bytes 3000000 | tf_op jit(solution)/shard_map/hyena_backward/pallas_call | solution.py:306
  81.7 1.1 %hand_over.1 = (bf16[128,1024]{1,0:T(8,128)(2,1)}, bf16[128,1024]{1,0:T(8,128)(2,1)}, bf16[128,1024]{1,0:T(8,128)(2,1)}, f32[128,1024]{1,0:T(8,128)}, f32[8,128]{1,0:T(8,128)}) custom-call(bf16[128,1024]{1,0:T(8,128)(2,1)S(1)} %get-tuple-element.15.refs_0_, bf16[128,1024]{1,0:T(8,128)(2,1)S(1)} %get-tuple-element.16.refs_1_, ...), custom_call_target="tpu_custom_call" | custom-call | bytes 3000000 | tf_op jit(solution)/shard_map/hand_over/pallas_call | solution.py:345

commit v6 on v5

--- a/solution.py
+++ b/solution.py
@@ -19,6 +19,7 @@
 GROUP = 4
 ROWS = GROUP * HALF
 Z_ORDER = (4, 3, 5, 2, 6, 1, 7)
+LATE_Y = 3
 
 
 @functools.cache
@@ -116,6 +117,33 @@
     def send_signal(s):
         send_near(s)
         send_far(s)
+
+    def send_last(s):
+        def early(j, carry):
+            for zi, dz in enumerate((*Z_ORDER, 0)):
+                xy = (j + zi) % 8
+                x, y = (my_x + xy // 4) % 2, (my_y + xy) % 4
+                there = x * 32 + planes[dz] + y
+
+                @pl.when((there != me) & ((x == 0) | (y < LATE_Y)))
+                def _():
+                    send_one(s, there)
+
+            return carry
+
+        def late(j, carry):
+            for zi, dz in enumerate((*Z_ORDER, 0)):
+                there = 32 + planes[dz] + LATE_Y + (j + zi) % (4 - LATE_Y)
+
+                @pl.when(there != me)
+                def _():
+                    send_one(s, there)
+
+            return carry
+
+        lax.fori_loop(0, 8, early, 0)
+        lax.fori_loop(0, 4 - LATE_Y, late, 0)
+        landed[s, rows_of(me), :] = leaving[s, rows_of(me), :]
 
     def wait_bytes(s, sems):
         most = pl.ds(0, (BLOCKS - 1) * OWN)
@@ -254,7 +282,7 @@
     inverse(1, 0, 2, True)
     send_signal(4)
     inverse(2, 1, 2, True)
-    send_signal(5)
+    send_last(5)
 
     wait_bytes(3, recv_sems)
     for j in range(WIDTH // LANES):

time: 83.2 us -> 82.8 us (level)
  no operation moved by 1% of the time
where the time goes in v6:
time: 82.8 us; the launch traced here: 82.3 us
  Pallas kernels  81.5 us (98%)
    pallas_call x1, Pallas kernels, on_device(): pl.pallas_call(kernel, out_shape=[pltpu.VMEM(out.shape, out.dtype) for ou...  80.4 us

profile of v6, /device:TPU:6, one launch (start us, length us, event | category | flops | bytes accessed | tf_op | source)
XLA Modules:
  0.0 82.3 jit_solution(14916726790020361881)
XLA Ops:
  0.6 80.4 %hyena_backward.1 = (bf16[128,1024]{1,0:T(8,128)(2,1)S(1)}, bf16[128,1024]{1,0:T(8,128)(2,1)S(1)}, bf16[128,1024]{1,0:T(8,128)(2,1)S(1)}, f32[128,1024]{1,0:T(8,128)S(1)}, f32[8,128]{1,0:T(8,128)S(1)}) custom-call(bf16[128,1024]{1,0:T(8,128)(2,1)} %query_hbm.1, bf16[128,1024]{1,0:T(8,128)(2,1)} %key_hbm.1, bf16[128,1024]{1,0:T(8,128)(2,1)} %value_hbm.1, ...), custom_call_target="tpu_custom_call" | custom-call | flops 4000000000 | bytes 3000000 | tf_op jit(solution)/shard_map/hyena_backward/pallas_call | solution.py:334
  81.0 1.1 %hand_over.1 = (bf16[128,1024]{1,0:T(8,128)(2,1)}, bf16[128,1024]{1,0:T(8,128)(2,1)}, bf16[128,1024]{1,0:T(8,128)(2,1)}, f32[128,1024]{1,0:T(8,128)}, f32[8,128]{1,0:T(8,128)}) custom-call(bf16[128,1024]{1,0:T(8,128)(2,1)S(1)} %get-tuple-element.15.refs_0_, bf16[128,1024]{1,0:T(8,128)(2,1)S(1)} %get-tuple-element.16.refs_1_, ...), custom_call_target="tpu_custom_call" | custom-call | bytes 3000000 | tf_op jit(solution)/shard_map/hand_over/pallas_call | solution.py:373

commit v7 on v6

--- a/solution.py
+++ b/solution.py
@@ -342,8 +342,8 @@
             pltpu.VMEM((1, WIDTH), f32),
             pltpu.VMEM(matrices.shape, f32),
             pltpu.VMEM(twists.shape, f32),
-            pltpu.VMEM((6, WIDTH, LANES), f32),
-            pltpu.VMEM((6, WIDTH, LANES), f32),
+            pltpu.VMEM((6, WIDTH + OWN, LANES), f32),
+            pltpu.VMEM((6, WIDTH + OWN, LANES), f32),
             pltpu.VMEM((3, OWN * HALF, 2 * LANES), f32),
             pltpu.VMEM((10, 1, LANES), f32),
             pltpu.VMEM((3, 8, 1, LANES), f32),

time: 82.8 us -> 82.8 us (level)
  no operation moved by 1% of the time
where the time goes in v7:
time: 82.8 us; the launch traced here: 82.3 us
  Pallas kernels  81.5 us (98%)
    pallas_call x1, Pallas kernels, on_device(): pl.pallas_call(kernel, out_shape=[pltpu.VMEM(out.shape, out.dtype) for ou...  80.4 us

profile of v7, /device:TPU:6, one launch (start us, length us, event | category | flops | bytes accessed | tf_op | source)
XLA Modules:
  0.0 82.3 jit_solution(1739952237028684207)
XLA Ops:
  0.6 80.4 %hyena_backward.1 = (bf16[128,1024]{1,0:T(8,128)(2,1)S(1)}, bf16[128,1024]{1,0:T(8,128)(2,1)S(1)}, bf16[128,1024]{1,0:T(8,128)(2,1)S(1)}, f32[128,1024]{1,0:T(8,128)S(1)}, f32[8,128]{1,0:T(8,128)S(1)}) custom-call(bf16[128,1024]{1,0:T(8,128)(2,1)} %query_hbm.1, bf16[128,1024]{1,0:T(8,128)(2,1)} %key_hbm.1, bf16[128,1024]{1,0:T(8,128)(2,1)} %value_hbm.1, ...), custom_call_target="tpu_custom_call" | custom-call | flops 4000000000 | bytes 3000000 | tf_op jit(solution)/shard_map/hyena_backward/pallas_call | solution.py:334
  81.0 1.1 %hand_over.1 = (bf16[128,1024]{1,0:T(8,128)(2,1)}, bf16[128,1024]{1,0:T(8,128)(2,1)}, bf16[128,1024]{1,0:T(8,128)(2,1)}, f32[128,1024]{1,0:T(8,128)}, f32[8,128]{1,0:T(8,128)}) custom-call(bf16[128,1024]{1,0:T(8,128)(2,1)S(1)} %get-tuple-element.15.refs_0_, bf16[128,1024]{1,0:T(8,128)(2,1)S(1)} %get-tuple-element.16.refs_1_, ...), custom_call_target="tpu_custom_call" | custom-call | bytes 3000000 | tf_op jit(solution)/shard_map/hand_over/pallas_call | solution.py:373
